TPU v7x, 128 devices: a whole 4x4x4 slice. The times are simulated.
128 devices in a mesh: lat: 16 (over z, y), chan: 8 (over x, core).
Axes of the slice: x: 4, y: 4, z: 4, core: 2. Of those that a mesh axis runs over, the one named last changes fastest.
Arguments:
- grid_in: bfloat16 [1, 720, 256, 1440], P(None, 'lat', 'chan'), may hold values from -6 to 6
- lat_weights: float32 [720], P('lat'), may hold values from 0.25 to 4
- legendre_basis: bfloat16 [192, 385, 720], P('lat'), may hold values from -0.21875 to 0.21875
- pair_list: int32 [192], replicated, may hold values from 0 to 191, each once
- filter_weights: bfloat16 [384, 256, 256], P(None, 'chan'), may hold values from -0.375 to 0.375
- cotangent: bfloat16 [1, 720, 256, 1440], P(None, 'lat', 'chan'), may hold values from -6 to 6
Outputs:
- block_out: bfloat16 [1, 720, 256, 1440], P(None, 'lat', 'chan')
- weight_grad: float32 [384, 256, 256], P('lat', 'chan')
Inputs may be any that keep to these rules, and one draw needn't show every extreme that they name: pair_list holds each of the 192 pairs of orders once; slot k pairs order pair_list[k] with order 384 - 1 - pair_list[k].
All inputs are finite; a program needn't handle non-finite values.
Results may differ from a plain program's by a relative error of at most 0.033.
Values may be sent and summed in bfloat16 or wider, within the bound.
No kernel may reach another device: no remote copies, remote signals or barrier semaphores. Data moves between devices by JAX's collectives and lax.ppermute only.
A program may use at most 192 MiB of HBM per device.

v0:
```python
import math

import jax
import jax.numpy as jnp
from jax import lax
from jax.sharding import PartitionSpec as P


def split_table(orders, lon_count, weights, lat_count, pairs_here):
    positions = jnp.arange(lon_count, dtype=jnp.int32)
    phases = orders[:, None] * positions[None, :] % lon_count
    angles = phases.astype(jnp.float32) * (2.0 * math.pi / lon_count)
    twiddle = jnp.stack([jnp.cos(angles), -jnp.sin(angles)], axis=1) * weights[:, None, None]
    high_part = twiddle.astype(jnp.bfloat16)
    low_part = (twiddle - high_part.astype(jnp.float32)).astype(jnp.bfloat16)
    shape = (lat_count, pairs_here, 2, 2, lon_count)
    return (high_part.reshape(shape), low_part.reshape(shape))


def to_spectrum(values, high_part, low_part):
    return jnp.einsum(
        "btcn,gkwin->gktwibc", values, high_part, preferred_element_type=jnp.float32
    ) + jnp.einsum("btcn,gkwin->gktwibc", values, low_part, preferred_element_type=jnp.float32)


def analysis(legendre_basis, spectra, first_orders, degrees):
    pairs_here = spectra.shape[0]
    row_index = jnp.arange(degrees + 1, dtype=jnp.int32)
    upper_rows = row_index[None, :] < (degrees - first_orders)[:, None]
    products = jnp.einsum(
        "krt,kty->kry", legendre_basis, spectra, preferred_element_type=jnp.float32
    )
    products = products.reshape(pairs_here, degrees + 1, 2, -1)
    return jnp.where(upper_rows[:, :, None], products[:, :, 0], products[:, :, 1])


def degree_table(packed, first_orders, degrees):

    def lower_part(block_rows, offset):
        padded = jnp.concatenate(
            [jnp.zeros((degrees,) + block_rows.shape[1:], block_rows.dtype), block_rows], axis=0
        )
        return lax.dynamic_slice_in_dim(padded, degrees - offset, degrees, 0)

    leading = jax.vmap(lower_part)(packed, first_orders)
    degree_index = jnp.arange(degrees, dtype=jnp.int32)
    keep_rows = degree_index[None, :] >= (degrees - 1 - first_orders)[:, None]
    trailing = jnp.where(
        keep_rows[:, :, None, None, None], packed[:, 1:], jnp.zeros((), packed.dtype)
    )
    return jnp.stack([leading, trailing], axis=1)


def packed_table(by_degree, first_orders, degrees):

    def upper_part(block_rows, offset):
        padded = jnp.concatenate(
            [block_rows, jnp.zeros((degrees + 1,) + block_rows.shape[1:], block_rows.dtype)], axis=0
        )
        return lax.dynamic_slice_in_dim(padded, offset, degrees + 1, 0)

    leading = jax.vmap(upper_part)(by_degree[:, 0], first_orders)
    trailing = by_degree[:, 1]
    trailing = jnp.concatenate([jnp.zeros_like(trailing[:, :1]), trailing], axis=1)
    return jnp.stack([leading, trailing], axis=1)


def on_device(grid_in, lat_weights, legendre_basis, pair_list, filter_weights, cotangent):
    lat_count = lax.axis_size("lat")
    owner_index = lax.axis_index("lat")
    pairs_here = legendre_basis.shape[0]
    degrees = legendre_basis.shape[1] - 1
    lat_total = legendre_basis.shape[2]
    batch_size, lat_rows, chan_rows, lon_count = grid_in.shape
    orders = jnp.stack([pair_list, degrees - 1 - pair_list], axis=1).reshape(-1)
    first_orders = lax.dynamic_slice_in_dim(pair_list, owner_index * pairs_here, pairs_here)
    lon_scale = 1.0 / math.sqrt(lon_count)
    forward_high, forward_low = split_table(
        orders, lon_count, jnp.full((degrees,), lon_scale, jnp.float32), lat_count, pairs_here
    )
    back_weights = jnp.where(orders == 0, 1.0, 2.0).astype(jnp.float32) * lon_scale
    inverse_high, inverse_low = split_table(orders, lon_count, back_weights, lat_count, pairs_here)
    transform = to_spectrum(grid_in, forward_high, forward_low)
    spectrum = (transform * lat_weights[None, None, :, None, None, None, None]).astype(jnp.bfloat16)
    spectrum = spectrum.reshape(lat_count, pairs_here, lat_rows, -1)
    arrived = lax.all_to_all(spectrum, "lat", split_axis=0, concat_axis=2, tiled=True)
    arrived = arrived.reshape(pairs_here, lat_total, -1)
    coefficients = analysis(legendre_basis, arrived, first_orders, degrees).astype(jnp.bfloat16)
    coefficients = coefficients.reshape(pairs_here, degrees + 1, 2, batch_size, chan_rows)
    all_coeffs = lax.all_gather(coefficients, "chan", axis=4, tiled=True)
    by_degree = degree_table(all_coeffs, first_orders, degrees)
    filtered = jnp.einsum(
        "loc,kwlibc->kwlibo", filter_weights, by_degree, preferred_element_type=jnp.float32
    ).astype(jnp.bfloat16)
    rows_packed = packed_table(filtered, first_orders, degrees)
    row_lines = jnp.swapaxes(rows_packed, 1, 2).reshape(pairs_here, degrees + 1, -1)
    synthesis = jnp.einsum(
        "krt,kry->kty", legendre_basis, row_lines, preferred_element_type=jnp.float32
    ).astype(jnp.bfloat16)
    synthesis = synthesis.reshape(pairs_here, lat_count, lat_rows, -1)
    returned = lax.all_to_all(synthesis, "lat", split_axis=1, concat_axis=0, tiled=True)
    returned = returned.reshape(lat_count, pairs_here, lat_rows, 2, 2, batch_size, chan_rows)
    grid_field = jnp.einsum(
        "gktwibo,gkwin->bton", returned, inverse_high, preferred_element_type=jnp.float32
    ) + jnp.einsum("gktwibo,gkwin->bton", returned, inverse_low, preferred_element_type=jnp.float32)
    block_out = (grid_in.astype(jnp.float32) + jax.nn.gelu(grid_field)).astype(jnp.bfloat16)
    pullback = jax.vjp(jax.nn.gelu, grid_field)[1]
    field_grad = pullback(cotangent.astype(jnp.float32))[0].astype(jnp.bfloat16)
    grad_spectrum = to_spectrum(field_grad, inverse_high, inverse_low).astype(jnp.bfloat16)
    grad_spectrum = grad_spectrum.reshape(lat_count, pairs_here, lat_rows, -1)
    grad_arrived = lax.all_to_all(grad_spectrum, "lat", split_axis=0, concat_axis=2, tiled=True)
    grad_arrived = grad_arrived.reshape(pairs_here, lat_total, -1)
    coefficient_grad = analysis(legendre_basis, grad_arrived, first_orders, degrees).astype(
        jnp.bfloat16
    )
    coefficient_grad = coefficient_grad.reshape(pairs_here, degrees + 1, 2, batch_size, chan_rows)
    degree_grad = degree_table(coefficient_grad, first_orders, degrees)
    weight_grad = lax.psum_scatter(
        jnp.einsum(
            "kwlibo,kwlibc->loc", degree_grad, by_degree, preferred_element_type=jnp.float32
        ).astype(jnp.bfloat16),
        "lat",
        scatter_dimension=0,
        tiled=True,
    ).astype(jnp.float32)
    return (block_out, weight_grad)


def solution(mesh):
    in_specs = (
        P(None, "lat", "chan", None),
        P("lat"),
        P("lat", None, None),
        P(),
        P(None, "chan", None),
        P(None, "lat", "chan", None),
    )
    out_specs = (P(None, "lat", "chan", None), P("lat", "chan", None))
    return jax.shard_map(
        on_device, mesh=mesh, in_specs=in_specs, out_specs=out_specs, check_vma=False
    )
```

profile of v0, /device:TPU:0, one launch (start us, length us, event | category | flops | bytes accessed | tf_op | source)
XLA Modules:
  0.0 633.1 jit_solution(9516492641369199072)
XLA Ops:
  8.8 9.9 %fusion.47 = (f32[16,12,2,1,1440]{4,0,3,2,1:T(8,128)S(1)}, f32[16,12,2,1,1440]{4,0,3,2,1:T(8,128)S(1)}) fusion(s32[16,12,2]{0,2,1:T(2,128)S(1)} %copy.121), kind=kLoop, calls=%fused_computation.64 | loop fusion | flops 5529600 | bytes 4425216 | tf_op jit(solution)/shard_map/cos | solution.py:13
  18.8 10.7 %fusion.20 = f32[16,12,2,2,45,32]{4,0,5,3,2,1:T(8,128)S(1)} fusion(bf16[45,32,1440,1,1,1]{2,1,0,5,4,3:T(8,128)(2,1)S(1)} %bitcast.183, f32[16,12,2,1,1440]{4,0,3,2,1:T(8,128)S(1)} %get-tuple-element.21, f32[16,12,2,1,1440]{4,0,3,2,1:T(8,128)S(1)} %get-tuple-element.20), kind=kOutput, calls=%fused_computation.41 | convolution fusion | flops 3191685120 | bytes 12994560 | tf_op jit(solution)/shard_map/btcn,gkwin->gktwibc/dot_general | solution.py:23
  29.4 18.7 %fusion.2 = bf16[16,12,2,2,1,45,32]{5,0,6,3,2,1,4:T(8,128)(2,1)} fusion(f32[16,12,2,2,45,32]{4,0,5,3,2,1:T(8,128)S(1)} %fusion.20, f32[45]{0:T(128)S(1)} %copy-done.13, bf16[45,32,1440,1,1,1]{2,1,0,5,4,3:T(8,128)(2,1)S(1)} %bitcast.184, f32[16,12,2,1,1440]{4,0,3,2,1:T(8,128)S(1)} %get-tuple-element.21, f32[16,12,2,1,1440]{4,0,3,2,1:T(8,128)S(1)} %get-tuple-element.20), kind=kOutput, calls=%fused_computation.10 | convolution fusion | flops 3191685120 | bytes 15206580 | tf_op jit(solution)/shard_map/btcn,gkwin->gktwibc/dot_general | solution.py:21
  48.1 8.1 %copy.125 = bf16[16,12,45,128]{3,2,1,0:T(8,128)(2,1)} copy(bf16[16,12,45,128]{2,0,3,1:T(8,128)(2,1)} %bitcast.172) | data formatting | bytes 4423680 | tf_op jit(solution)/shard_map/reshape | solution.py:85
  56.2 8.1 %all-to-all-start = ((bf16[16,12,45,128]{3,2,1,0:T(8,128)(2,1)}), bf16[16,12,45,128]{3,2,1,0:T(8,128)(2,1)S(1)}, u32[]{:S(2)}, u32[]{:S(2)}) async-start(bf16[16,12,45,128]{3,2,1,0:T(8,128)(2,1)} %copy.125), calls=%async_computation | async-start | bytes 4718592 | tf_op jit(solution)/shard_map/all_to_all | solution.py:86
  64.5 35.3 %all-to-all-done = bf16[16,12,45,128]{3,2,1,0:T(8,128)(2,1)S(1)} async-done(((bf16[16,12,45,128]{3,2,1,0:T(8,128)(2,1)}), bf16[16,12,45,128]{3,2,1,0:T(8,128)(2,1)S(1)}, u32[]{:S(2)}, u32[]{:S(2)}) %all-to-all-start) | async-done | bytes 2211872 | tf_op jit(solution)/shard_map/all_to_all | solution.py:86
  99.8 2.0 copy.126
  101.8 2.7 reshape.268
  104.5 5.1 convolution_bitcast_fusion.1
  113.0 38.9 %all-gather.2.cloned.1.call-done = bf16[12,385,2,1,256]{1,2,3,0,4:T(2,128)(2,1)} async-done(((bf16[12,385,2,1,32]{1,2,3,0,4:T(2,128)(2,1)}), bf16[12,385,2,1,256]{1,2,3,0,4:T(2,128)(2,1)}) %all-gather.2.cloned.1.call-update) | async-done | bytes 4730896 | tf_op jit(solution)/shard_map/all_gather | solution.py:90
  151.8 13.7 %slice.55 = bf16[12,384,2,1,256]{1,2,3,0,4:T(2,128)(2,1)} slice(bf16[12,385,2,1,256]{1,2,3,0,4:T(2,128)(2,1)} %all-gather.2.cloned.1.call-done), slice={[0:12], [1:385], [0:2], [0:1], [0:256]} | slice | bytes 9437184 | tf_op jit(solution)/shard_map/slice | solution.py:49
  165.5 12.5 %copy.178 = bf16[12,384,2,1,256]{4,0,2,1,3:T(8,128)(2,1)} copy(bf16[12,384,2,1,256]{1,2,3,0,4:T(2,128)(2,1)} %slice.55) | data formatting | bytes 9437184
  178.0 21.1 %copy.131 = bf16[12,385,2,1,256]{4,2,3,0,1:T(2,128)(2,1)} copy(bf16[12,385,2,1,256]{1,2,3,0,4:T(2,128)(2,1)} %all-gather.2.cloned.1.call-done) | data formatting | bytes 9461760 | tf_op jit(solution)/shard_map/all_gather | solution.py:90
  199.1 19.0 %concatenate.25 = bf16[12,769,2,1,256]{4,2,3,0,1:T(2,128)(2,1)} pad(bf16[12,385,2,1,256]{4,2,3,0,1:T(2,128)(2,1)} %copy.131, bf16[]{:T(256)} %constant.13.clone.1), padding=0_0x384_0x0_0x0_0x0_0 | pad | bytes 14180354 | tf_op jit(solution)/shard_map/vmap()/concatenate | solution.py:40
  218.2 16.4 %gather_fusion = bf16[12,384,2,256]{3,2,1,0:T(2,128)(2,1)} fusion(bf16[12,769,2,1,256]{4,2,3,0,1:T(2,128)(2,1)} %concatenate.25, s32[12]{0:T(128)S(1)} %fusion.55), kind=kCustom, calls=%fused_computation | custom fusion | bytes 9437424 | tf_op jit(solution)/shard_map/vmap()/gather | solution.py:43
  234.6 10.4 %copy.200 = bf16[12,384,2,256]{3,0,2,1:T(8,128)(2,1)} copy(bf16[12,384,2,256]{3,2,1,0:T(2,128)(2,1)} %gather_fusion) | data formatting | bytes 9437184 | tf_op jit(solution)/shard_map/vmap()/gather | solution.py:43
  245.0 3.3 select_bitcast_fusion
  248.3 8.6 %convert_bitcast_fusion = bf16[12,2,384,2,1,32]{5,0,3,1,2,4:T(8,128)(2,1)S(1)} fusion(bf16[384,32,256]{2,1,0:T(8,128)(2,1)} %param.10, bf16[12,1,384,2,1,256]{5,0,3,1,2,4:T(8,128)(2,1)} %select_bitcast_fusion, bf16[12,1,384,2,1,256]{5,0,3,1,2,4:T(8,128)(2,1)} %bitcast.175), kind=kOutput, calls=%fused_computation.30 | convolution fusion | flops 307298304 | bytes 16908288 | tf_op jit(solution)/shard_map/loc,kwlibc->kwlibo/dot_general | solution.py:92
  256.9 2.9 slice_bitcast_fusion.1
  259.7 2.4 copy.179
  262.2 5.8 concatenate.27.clone
  268.0 12.2 %gather_fusion.1 = bf16[12,385,2,32]{3,2,1,0:T(2,128)(2,1)S(1)} fusion(bf16[12,769,2,1,32]{4,2,3,0,1:T(2,128)(2,1)} %concatenate.27.clone, s32[12]{0:T(128)S(1)} %get-tuple-element.12), kind=kCustom, calls=%fused_computation.1 | custom fusion | bytes 1182960 | tf_op jit(solution)/shard_map/vmap()/gather | solution.py:60
  280.2 4.8 copy.136
  285.0 2.6 pad_bitcast_fusion
  287.6 3.9 copy.137
  293.1 7.3 %convert_bitcast_fusion.1 = bf16[12,720,128]{2,1,0:T(8,128)(2,1)} fusion(bf16[12,385,128]{1,2,0:T(8,128)(2,1)S(1)} %bitcast.177, bf16[12,385,720]{2,1,0:T(8,128)(2,1)} %param.8), kind=kOutput, calls=%fused_computation.66 | convolution fusion | flops 852664320 | bytes 10047360 | tf_op jit(solution)/shard_map/krt,kry->kty/dot_general | solution.py:97
  300.3 2.7 reshape.272
  303.0 2.0 copy.139
  305.1 7.0 %all-to-all-start.1 = ((bf16[12,16,45,128]{3,2,0,1:T(8,128)(2,1)}), bf16[12,16,45,128]{3,2,0,1:T(8,128)(2,1)S(1)}, u32[]{:S(2)}, u32[]{:S(2)}) async-start(bf16[12,16,45,128]{3,2,0,1:T(8,128)(2,1)} %copy.139), calls=%async_computation.1 | async-start | bytes 4718592 | tf_op jit(solution)/shard_map/all_to_all | solution.py:101
  312.2 37.0 %all-to-all-done.1 = bf16[12,16,45,128]{3,2,0,1:T(8,128)(2,1)S(1)} async-done(((bf16[12,16,45,128]{3,2,0,1:T(8,128)(2,1)}), bf16[12,16,45,128]{3,2,0,1:T(8,128)(2,1)S(1)}, u32[]{:S(2)}, u32[]{:S(2)}) %all-to-all-start.1) | async-done | bytes 2211872 | tf_op jit(solution)/shard_map/all_to_all | solution.py:101
  349.2 6.4 %reshape.324 = bf16[16,12,45,2,2,32]{5,4,3,2,1,0:T(2,128)(2,1)} reshape(bf16[16,12,1,45,128]{4,3,1,0,2:T(8,128)(2,1)S(1)} %bitcast.170) | data formatting | bytes 4423680 | tf_op jit(solution)/shard_map/reshape.10
  355.7 30.4 %copy.141 = bf16[16,12,45,2,2,32]{2,0,4,5,3,1:T(8,128)(2,1)} copy(bf16[16,12,45,2,2,32]{5,4,3,2,1,0:T(2,128)(2,1)} %reshape.324) | data formatting | bytes 4423680 | tf_op jit(solution)/shard_map/reshape.10
  386.1 11.2 %fusion.41 = f32[1440,45,32,1,1,1]{0,1,3,2,5,4:T(8,128)} fusion(bf16[16,12,45,2,2,32]{2,0,4,5,3,1:T(8,128)(2,1)} %copy.141, f32[16,12,2]{0,2,1:T(2,128)S(1)} %copy.122, f32[16,12,2,1,1440]{4,0,3,2,1:T(8,128)} %copy-done.2, f32[16,12,2,1,1440]{4,0,3,2,1:T(8,128)S(1)} %copy-done.1), kind=kOutput, calls=%fused_computation.56 | convolution fusion | flops 3188367360 | bytes 14931456 | tf_op jit(solution)/shard_map/gktwibo,gkwin->bton/dot_general | solution.py:103
  397.3 18.7 %add_convert_fusion.1 = (bf16[1,45,32,1440]{3,1,2,0:T(8,128)(2,1)}, f32[1,45,32,1440]{3,1,2,0:T(8,128)}) fusion(bf16[1,45,32,1440]{3,2,1,0:T(8,128)(2,1)} %param.6, bf16[16,12,45,2,2,32]{2,0,4,5,3,1:T(8,128)(2,1)} %copy.141, f32[16,12,2]{0,2,1:T(2,128)S(1)} %copy.122, f32[16,12,2,1,1440]{4,0,3,2,1:T(8,128)} %copy-done.2, ...), kind=kOutput, calls=%fused_computation.26 | convolution fusion | flops 3216568320 | bytes 31520256 | tf_op jit(solution)/shard_map/gktwibo,gkwin->bton/dot_general | solution.py:105
  416.0 17.4 %fusion.16 = f32[16,12,2,2,45,32]{4,0,5,3,2,1:T(8,128)} fusion(f32[16,12,2]{0,2,1:T(2,128)S(1)} %copy.122, f32[16,12,2,1,1440]{4,0,3,2,1:T(8,128)} %copy-done.2, f32[16,12,2,1,1440]{4,0,3,2,1:T(8,128)S(1)} %copy-done.1, f32[1,45,32,1440]{3,1,2,0:T(8,128)} %get-tuple-element.25, bf16[1,45,32,1440]{3,2,1,0:T(8,128)(2,1)} %param.11), kind=kOutput, calls=%fused_computation.33 | convolution fusion | flops 3235230720 | bytes 21290496 | tf_op jit(solution)/shard_map/btcn,gkwin->gktwibc/dot_general | solution.py:23
  433.4 15.8 %add_convert_fusion = bf16[16,12,2,2,45,32]{4,0,5,3,2,1:T(8,128)(2,1)} fusion(f32[16,12,2,2,45,32]{4,0,5,3,2,1:T(8,128)} %fusion.16, f32[16,12,2]{0,2,1:T(2,128)S(1)} %copy.122, f32[16,12,2,1,1440]{4,0,3,2,1:T(8,128)S(1)} %copy-done.3, f32[16,12,2,1,1440]{4,0,3,2,1:T(8,128)S(1)} %copy-done.1, f32[1,45,32,1440]{3,1,2,0:T(8,128)S(1)} %copy-done.14, ...), kind=kOutput, calls=%fused_computation.11 | convolution fusion | flops 3234124800 | bytes 23502336 | tf_op jit(solution)/shard_map/btcn,gkwin->gktwibc/dot_general | solution.py:21
  449.2 7.1 %copy.144 = bf16[16,12,45,128]{3,2,1,0:T(8,128)(2,1)S(1)} copy(bf16[16,12,45,128]{2,0,3,1:T(8,128)(2,1)} %bitcast.171) | data formatting | bytes 4423680 | tf_op jit(solution)/shard_map/reshape | solution.py:110
  456.4 34.6 %all_to_all.45 = bf16[16,12,45,128]{3,2,1,0:T(8,128)(2,1)S(1)} all-to-all(bf16[16,12,45,128]{3,2,1,0:T(8,128)(2,1)S(1)} %copy.144), channel_id=1, replica_groups=mesh['lat'=16,'chan'=8] {'lat'}, dimensions={0} | all-to-all | bytes 4423680 | tf_op jit(solution)/shard_map/all_to_all | solution.py:111
  491.5 2.2 reshape.276
  493.7 5.7 convolution_bitcast_fusion
  501.5 3.6 copy.180
  505.2 5.7 concatenate.30.clone
  510.9 11.8 %gather_fusion.2 = bf16[12,384,2,32]{3,2,1,0:T(2,128)(2,1)S(1)} fusion(bf16[12,769,2,1,32]{4,2,3,0,1:T(2,128)(2,1)} %concatenate.30.clone, s32[12]{0:T(128)S(1)} %copy-done.6), kind=kCustom, calls=%fused_computation.2 | custom fusion | bytes 1179888 | tf_op jit(solution)/shard_map/vmap()/gather | solution.py:43
  524.6 9.3 %copy.167 = bf16[12,2,384,2,32]{4,0,1,3,2:T(8,128)(2,1)} copy(bf16[12,2,384,2,32]{2,4,3,0,1:T(8,128)(2,1)S(1)} %maximum_bitcast_fusion.1) | data formatting | bytes 2359296 | tf_op jit(solution)/shard_map/reshape.38
  533.9 11.6 %bitcast_convert_fusion = bf16[384,32,256]{2,1,0:T(8,128)(2,1)} fusion(bf16[12,2,384,2,32]{4,0,1,3,2:T(8,128)(2,1)} %copy.167, bf16[12,1,384,2,1,256]{5,0,3,1,2,4:T(8,128)(2,1)} %select_bitcast_fusion, bf16[12,1,384,2,1,256]{5,0,3,1,2,4:T(8,128)(2,1)} %bitcast.176), kind=kOutput, calls=%fused_computation.6 | convolution fusion | flops 309854208 | bytes 16908288 | tf_op jit(solution)/shard_map/kwlibo,kwlibc->loc/dot_general | solution.py:119
  545.5 6.9 %copy.153 = bf16[1,45,32,1440]{3,2,1,0:T(8,128)(2,1)} copy(bf16[1,45,32,1440]{3,1,2,0:T(8,128)(2,1)} %get-tuple-element.24) | data formatting | bytes 8294400
  552.4 71.4 %reduce-scatter.2.cloned.1.call-done = bf16[24,32,256]{2,1,0:T(8,128)(2,1)} async-done(((bf16[384,32,256]{2,1,0:T(8,128)(2,1)}), bf16[24,32,256]{2,1,0:T(8,128)(2,1)}) %reduce-scatter.2.cloned.1.call-update) | async-done | bytes 393232 | tf_op jit(solution)/shard_map/reduce_scatter | solution.py:118
  623.8 2.0 convert_element_type.135
  (65 shorter events, 11.3 us)
Async XLA Ops:
  8.8 9.9 %copy-start.12 = (bf16[1,45,32,1440]{3,2,1,0:T(8,128)(2,1)S(1)}, bf16[1,45,32,1440]{3,2,1,0:T(8,128)(2,1)}, u32[]{:S(2)}) copy-start(bf16[1,45,32,1440]{3,2,1,0:T(8,128)(2,1)} %param.6) | copy-start | bytes 12441604
  18.7 10.7 %copy-start = (f32[16,12,2,1,1440]{4,0,3,2,1:T(8,128)}, f32[16,12,2,1,1440]{4,0,3,2,1:T(8,128)S(1)}, u32[]{:S(2)}) copy-start(f32[16,12,2,1,1440]{4,0,3,2,1:T(8,128)S(1)} %get-tuple-element.20) | copy-start | bytes 6635524
  18.7 10.7 %copy-start.2 = (f32[16,12,2,1,1440]{4,0,3,2,1:T(8,128)}, f32[16,12,2,1,1440]{4,0,3,2,1:T(8,128)S(1)}, u32[]{:S(2)}) copy-start(f32[16,12,2,1,1440]{4,0,3,2,1:T(8,128)S(1)} %get-tuple-element.21) | copy-start | bytes 6635524
  18.7 10.7 %copy-start.13 = (f32[45]{0:T(128)S(1)}, f32[45]{0:T(128)}, u32[]{:S(2)}) copy-start(f32[45]{0:T(128)} %param.7) | copy-start | bytes 544
  48.1 16.2 %copy-start.11 = (s32[192]{0:T(256)S(1)}, s32[192]{0:T(256)}, u32[]{:S(2)}) copy-start(s32[192]{0:T(256)} %param.9) | copy-start | bytes 2308
  56.2 43.6 %all-to-all-start = ((bf16[16,12,45,128]{3,2,1,0:T(8,128)(2,1)}), bf16[16,12,45,128]{3,2,1,0:T(8,128)(2,1)S(1)}, u32[]{:S(2)}, u32[]{:S(2)}) async-start(bf16[16,12,45,128]{3,2,1,0:T(8,128)(2,1)} %copy.125), calls=%async_computation | async-start | bytes 4718592 | tf_op jit(solution)/shard_map/all_to_all | solution.py:86
  64.3 87.5 %all-gather.2.cloned.1.call-start = ((), (), s32[]{:S(2)}) async-start(), calls=%async_computation.4 | async-start | bytes 7077888 | tf_op jit(solution)/shard_map/all_gather | solution.py:90
  64.5 46.3 %copy-start.7 = (pred[12,385]{1,0:T(8,128)(4,1)}, pred[12,385]{1,0:T(8,128)(4,1)S(1)}, u32[]{:S(2)}) copy-start(pred[12,385]{1,0:T(8,128)(4,1)S(1)} %iota_compare_fusion) | copy-start | bytes 13864
  112.8 52.8 %copy-start.9 = (pred[12,384]{1,0:T(8,128)(4,1)}, pred[12,384]{1,0:T(8,128)(4,1)S(1)}, u32[]{:S(2)}) copy-start(pred[12,384]{1,0:T(8,128)(4,1)S(1)} %iota_compare_fusion.1) | copy-start | bytes 13828
  113.0 105.2 %copy-start.5 = (s32[12]{0:T(128)}, s32[12]{0:T(128)S(1)}, u32[]{:S(2)}) copy-start(s32[12]{0:T(128)S(1)} %fusion.55) | copy-start | bytes 148
  218.2 26.8 %slice-start = ((s8[6291456]{0:T(1024)(128)(4,1)}), s8[2097152]{0:T(1024)(128)(4,1)S(1)}, s32[]{:S(2)}) async-start(s8[6291456]{0:T(1024)(128)(4,1)} %bitcast.165), calls=%async_computation.6 | async-start | bytes 4194304
  234.6 10.4 %slice-start.1 = ((s8[6291456]{0:T(1024)(128)(4,1)}), s8[4194304]{0:T(1024)(128)(4,1)S(1)}, s32[]{:S(2)}) async-start(s8[6291456]{0:T(1024)(128)(4,1)} %bitcast.165), calls=%async_computation.7 | async-start | bytes 8388608
  305.1 44.2 %all-to-all-start.1 = ((bf16[12,16,45,128]{3,2,0,1:T(8,128)(2,1)}), bf16[12,16,45,128]{3,2,0,1:T(8,128)(2,1)S(1)}, u32[]{:S(2)}, u32[]{:S(2)}) async-start(bf16[12,16,45,128]{3,2,0,1:T(8,128)(2,1)} %copy.139), calls=%async_computation.1 | async-start | bytes 4718592 | tf_op jit(solution)/shard_map/all_to_all | solution.py:101
  312.0 311.8 %reduce-scatter.2.cloned.1.call-start = ((), (), s32[]{:S(2)}) async-start(), calls=%async_computation.5 | async-start | bytes 6684672 | tf_op jit(solution)/shard_map/reduce_scatter | solution.py:118
  355.7 30.4 %copy-start.1 = (f32[16,12,2,1,1440]{4,0,3,2,1:T(8,128)S(1)}, f32[16,12,2,1,1440]{4,0,3,2,1:T(8,128)}, u32[]{:S(2)}) copy-start(f32[16,12,2,1,1440]{4,0,3,2,1:T(8,128)} %copy-done) | copy-start | bytes 6635524
  416.0 17.4 %copy-start.3 = (f32[16,12,2,1,1440]{4,0,3,2,1:T(8,128)S(1)}, f32[16,12,2,1,1440]{4,0,3,2,1:T(8,128)}, u32[]{:S(2)}) copy-start(f32[16,12,2,1,1440]{4,0,3,2,1:T(8,128)} %copy-done.2) | copy-start | bytes 6635524
  416.0 17.4 %copy-start.14 = (f32[1,45,32,1440]{3,1,2,0:T(8,128)S(1)}, f32[1,45,32,1440]{3,1,2,0:T(8,128)}, u32[]{:S(2)}) copy-start(f32[1,45,32,1440]{3,1,2,0:T(8,128)} %get-tuple-element.25) | copy-start | bytes 24883204
  499.4 0.9 copy-start.8
  499.5 1.0 copy-start.10
  501.5 9.4 %copy-start.6 = (s32[12]{0:T(128)S(1)}, s32[12]{0:T(128)}, u32[]{:S(2)}) copy-start(s32[12]{0:T(128)} %copy-done.5) | copy-start | bytes 148
  510.9 13.5 %copy-start.4 = (bf16[12,1,384,2,1,32]{2,5,3,0,4,1:T(8,128)(2,1)S(1)}, bf16[12,1,384,2,1,32]{2,5,3,0,4,1:T(8,128)(2,1)}, u32[]{:S(2)}) copy-start(bf16[12,1,384,2,1,32]{2,5,3,0,4,1:T(8,128)(2,1)} %fusion.49) | copy-start | bytes 1769476
Sparse Core Ops, SparseCore 0:
  112.8 38.9 all-gather.1
  545.6 78.1 reduce-scatter.1
where the time goes:
time: 644 us; the launch traced here: 633 us
  local copies, waits for them, and re-layouts  236 us (37%)
  waiting for transfers between devices  183 us (28%)
  matrix products  131 us (20%)
  blocking collectives  34.6 us (5%)
  other arithmetic  19.1 us (3%)
  starting transfers between devices  15.2 us (2%)
  between operations  14.9 us (2%)
    reduce_scatter x1, waiting for transfers between devices, on_device(): lax.psum_scatter(jnp.einsum('kwlibo,kwlibc->loc', degree_grad, by_degree,...  71.4 us
    another operation x3, local copies, waits for them, and re-layouts  46.2 us
    gather x4, local copies, waits for them, and re-layouts, lower_part(): return lax.dynamic_slice_in_dim(padded, degrees - offset, degrees, 0)  40.3 us
    all_gather x1, waiting for transfers between devices, on_device(): all_coeffs = lax.all_gather(coefficients, 'chan', axis=4, tiled=True)  38.9 us
    all_to_all x1, waiting for transfers between devices, on_device(): lax.all_to_all(synthesis, 'lat', split_axis=1, concat_axis=0, tiled=True)  37 us
    all_to_all x1, waiting for transfers between devices, on_device(): lax.all_to_all(spectrum, 'lat', split_axis=0, concat_axis=2, tiled=True)  35.3 us
    all_to_all x1, blocking collectives, on_device(): lax.all_to_all(grad_spectrum, 'lat', split_axis=0, concat_axis=2, tiled=T...  34.6 us
    dot_general x2, matrix products, to_spectrum(): jnp.einsum('btcn,gkwin->gktwibc', values, high_part, preferred_element_ty...  34.5 us
  transfers between devices with their start and end apart: 4, of which 4 were waited for; matrix products, arithmetic and copies ran while one was open for 1% of the time, Pallas kernels for 0%

commit v1 on v0

v1 whole, which is shorter than its diff:
```python
import functools
import math

import jax
import jax.numpy as jnp
import numpy as np
from jax import lax
from jax.experimental import pallas as pl
from jax.experimental.pallas import tpu as pltpu
from jax.sharding import PartitionSpec as P

F32 = jnp.float32
BF16 = jnp.bfloat16
GROUP = 32
T_STEP = 16
CHUNKS = ((0, 12),)


def params(mib=56):
    return pltpu.CompilerParams(vmem_limit_bytes=mib << 20)


def round_up(value, unit):
    return -(-value // unit) * unit


def longitude_table(degrees, lon_count, doubled):
    first = np.arange(degrees // 2)
    orders = np.stack([first, degrees - 1 - first])
    phases = orders[:, :, None] * np.arange(lon_count) % lon_count
    angles = phases * (2.0 * math.pi / lon_count)
    table = np.stack([np.cos(angles), -np.sin(angles)], axis=1) / math.sqrt(lon_count)
    if doubled:
        table = table * np.where(orders == 0, 1.0, 2.0)[:, None, :, None]
    return jnp.asarray(table.reshape(2 * degrees, lon_count).astype(np.float32)).astype(BF16)


def swap_groups(tiles):
    lane_group = lax.broadcasted_iota(jnp.int32, tiles[0].shape, 1) // GROUP
    swapped = []
    for s in range(4):
        total = None
        for a in range(4):
            shift = (a - s) % 4 * GROUP
            moved = pltpu.roll(tiles[a], shift, 1) if shift else tiles[a]
            total = moved if total is None else jnp.where(lane_group == a, moved, total)
        swapped.append(total)
    return swapped


P_BLOCK = 32


def by_latitude(rows_ref, stacked_ref, pairs, scale_ref):
    def step(block, _):
        start = pl.multiple_of(block * P_BLOCK, P_BLOCK)
        for q in range(T_STEP // 4):
            lanes = slice(128 * q, 128 * q + 128)
            tiles = [rows_ref[pl.ds(wi * pairs + start, P_BLOCK), lanes] for wi in range(4)]
            if scale_ref is not None:
                tiles = [tile * scale_ref[:, lanes] for tile in tiles]
            for s, tile in enumerate(swap_groups(tiles)):
                stacked_ref[pl.ds((4 * q + s) * pairs + start, P_BLOCK), :] = tile
        return 0

    lax.fori_loop(0, pairs // P_BLOCK, step, 0)


def by_order(stacked_ref, rows_ref, pairs):
    def step(block, _):
        start = pl.multiple_of(block * P_BLOCK, P_BLOCK)
        for q in range(T_STEP // 4):
            tiles = [
                stacked_ref[pl.ds((4 * q + s) * pairs + start, P_BLOCK), :] for s in range(4)
            ]
            for wi, tile in enumerate(swap_groups(tiles)):
                rows_ref[pl.ds(wi * pairs + start, P_BLOCK), 128 * q : 128 * q + 128] = tile.astype(
                    rows_ref.dtype
                )
        return 0

    lax.fori_loop(0, pairs // P_BLOCK, step, 0)


def send_slots(pair_ref, stacked_ref, out_refs, pairs, slots):
    for (low, high), out_ref in zip(CHUNKS, out_refs):

        def step(owner, _):
            for k in range(low, high):
                order = pair_ref[owner * slots + k]
                tile = stacked_ref[pl.ds(order, T_STEP, stride=pairs), :]
                out_ref[owner, k - low] = tile.astype(BF16)
            return 0

        lax.fori_loop(0, pairs // slots, step, 0)


def nt_dot(a, b):
    return lax.dot_general(a, b, (((1,), (1,)), ((), ())), preferred_element_type=F32)


def tn_dot(a, b):
    return lax.dot_general(a, b, (((0,), (0,)), ((), ())), preferred_element_type=F32)


def forward_body(pairs, slots, pair_ref, grid_ref, scale_ref, table_ref, *refs):
    out_refs = refs[: len(CHUNKS)]
    rows_ref, stacked_ref = refs[len(CHUNKS) :]
    fields = grid_ref[...].reshape(T_STEP * GROUP, -1)
    rows_ref[...] = nt_dot(table_ref[...], fields)
    by_latitude(rows_ref, stacked_ref, pairs, scale_ref)
    send_slots(pair_ref, stacked_ref, out_refs, pairs, slots)


def slot_specs(owners):
    return [
        pl.BlockSpec((owners, high - low, T_STEP, 128), lambda t: (0, 0, t, 0))
        for low, high in CHUNKS
    ]


def slot_shapes(owners, lat_rows):
    return [jax.ShapeDtypeStruct((owners, high - low, lat_rows, 128), BF16) for low, high in CHUNKS]


def forward_transform(grid, scale, pair_list, table, owners, slots):
    lat_rows, _, lon_count = grid.shape
    pairs = owners * slots
    return pl.pallas_call(
        functools.partial(forward_body, pairs, slots),
        grid=(pl.cdiv(lat_rows, T_STEP),),
        in_specs=[
            pl.BlockSpec(memory_space=pltpu.SMEM),
            pl.BlockSpec((T_STEP, GROUP, lon_count), lambda t: (t, 0, 0)),
            pl.BlockSpec((1, T_STEP * GROUP), lambda t: (0, t)),
            pl.BlockSpec((4 * pairs, lon_count), lambda t: (0, 0)),
        ],
        out_specs=slot_specs(owners),
        out_shape=slot_shapes(owners, lat_rows),
        scratch_shapes=[
            pltpu.VMEM((4 * pairs, T_STEP * GROUP), F32),
            pltpu.VMEM((T_STEP * pairs, 128), F32),
        ],
        compiler_params=params(),
        name="forward_transform",
    )(pair_list, grid, scale, table)


def middle_body(pairs, slots, pair_ref, *refs):
    count = len(CHUNKS)
    in_refs, refs = refs[:count], refs[count:]
    grid_ref, cot_ref, table_ref, out_ref = refs[:4]
    out_refs = refs[4 : 4 + count]
    rows_ref, stacked_ref, lines_ref, grad_ref = refs[4 + count :]
    for (low, high), in_ref in zip(CHUNKS, in_refs):

        def step(owner, _):
            for k in range(low, high):
                order = pair_ref[owner * slots + k]
                tile = in_ref[owner, k - low].astype(F32)
                stacked_ref[pl.ds(order, T_STEP, stride=pairs), :] = tile
            return 0

        lax.fori_loop(0, pairs // slots, step, 0)
    by_order(stacked_ref, lines_ref, pairs)
    root = math.sqrt(2.0 / math.pi)
    t_part = 4
    for q in range(T_STEP // t_part):
        rows = slice(128 * q, 128 * q + 128)
        lats = slice(t_part * q, t_part * q + t_part)
        x = tn_dot(lines_ref[:, rows], table_ref[...])
        square = x * x
        th = jnp.tanh(x * (root + (root * 0.044715) * square))
        half = 0.5 + 0.5 * th
        gate = x * half
        slope = half + gate * (1.0 - th) * (root + (3.0 * root * 0.044715) * square)
        grid = grid_ref[lats].reshape(128, -1).astype(F32)
        out_ref[lats] = (grid + gate).astype(BF16).reshape(t_part, GROUP, -1)
        cot = cot_ref[lats].reshape(128, -1).astype(F32)
        grad_ref[rows, :] = (cot * slope).astype(BF16)
    rows_ref[...] = nt_dot(table_ref[...], grad_ref[...])
    by_latitude(rows_ref, stacked_ref, pairs, None)
    send_slots(pair_ref, stacked_ref, out_refs, pairs, slots)


def middle_transform(returned, grid, cotangent, pair_list, table, owners, slots):
    lat_rows, _, lon_count = grid.shape
    pairs = owners * slots
    field_spec = pl.BlockSpec((T_STEP, GROUP, lon_count), lambda t: (t, 0, 0))
    return pl.pallas_call(
        functools.partial(middle_body, pairs, slots),
        grid=(pl.cdiv(lat_rows, T_STEP),),
        in_specs=[pl.BlockSpec(memory_space=pltpu.SMEM)]
        + slot_specs(owners)
        + [
            field_spec,
            field_spec,
            pl.BlockSpec((4 * pairs, lon_count), lambda t: (0, 0)),
        ],
        out_specs=[field_spec] + slot_specs(owners),
        out_shape=[jax.ShapeDtypeStruct(grid.shape, BF16)] + slot_shapes(owners, lat_rows),
        scratch_shapes=[
            pltpu.VMEM((4 * pairs, T_STEP * GROUP), F32),
            pltpu.VMEM((T_STEP * pairs, 128), F32),
            pltpu.VMEM((4 * pairs, T_STEP * GROUP), BF16),
            pltpu.VMEM((T_STEP * GROUP, lon_count), BF16),
        ],
        compiler_params=params(),
        name="middle_transform",
    )(pair_list, *returned, grid, cotangent, table)


def degree_starts(degrees, chans, block_rows, count):
    starts = []
    for tile in range(degrees // 8):
        owner, s = divmod(tile, degrees // 8 // 16)
        starts.append(owner * chans * block_rows + s * count)
    return starts


def analysis_body(degrees, low, count, block_rows, first_ref, in_ref, basis_ref, out_ref, *refs):
    lats_ref, rows_ref, sent_ref = refs
    k = pl.program_id(0)
    first = first_ref[low + k]
    owners, lat_rows = in_ref.shape[0], in_ref.shape[2]

    @pl.when(k == 0)
    def _():
        sent_ref[...] = jnp.zeros_like(sent_ref)

    for owner in range(owners):
        lats_ref[owner * lat_rows : (owner + 1) * lat_rows, :] = in_ref[owner, 0].astype(F32)
    spectrum = lats_ref[...].astype(BF16)
    rows_ref[: degrees + 1, :] = jnp.dot(basis_ref[0], spectrum, preferred_element_type=F32)
    rows_ref[degrees + 1 :, :] = jnp.zeros((7, 128), F32)
    leading = pltpu.roll(rows_ref[...], first, 0)[:degrees]
    trailing = rows_ref[1 : degrees + 1, :]
    degree = lax.broadcasted_iota(jnp.int32, (degrees, 128), 0)
    lane = lax.broadcasted_iota(jnp.int32, (degrees, 128), 1)
    is_first = lane < 64
    smallest = jnp.where(is_first, first, degrees - 1 - first)
    table = jnp.where(degree >= smallest, jnp.where(is_first, leading, trailing), 0.0)
    for tile, start in enumerate(degree_starts(degrees, 8, block_rows, count)):
        sent_ref[pl.ds(start + k, 8, stride=block_rows), :] = table[8 * tile : 8 * tile + 8]

    @pl.when(k == pl.num_programs(0) - 1)
    def _():
        out_ref[...] = sent_ref[...].astype(BF16).reshape(out_ref.shape)


def analysis(arrived, basis, firsts, chunk):
    low, high = chunk
    count = high - low
    owners, _, lat_rows, _ = arrived.shape
    slots, rows, lat_total = basis.shape
    degrees = rows - 1
    block_rows = round_up(3 * count, 8)
    return pl.pallas_call(
        functools.partial(analysis_body, degrees, low, count, block_rows),
        grid=(count,),
        in_specs=[
            pl.BlockSpec(memory_space=pltpu.SMEM),
            pl.BlockSpec((owners, 1, lat_rows, 128), lambda k: (0, k, 0, 0)),
            pl.BlockSpec((1, rows, lat_total), lambda k: (low + k, 0, 0)),
        ],
        out_specs=pl.BlockSpec((128, block_rows, 128), lambda k: (0, 0, 0)),
        out_shape=jax.ShapeDtypeStruct((128, block_rows, 128), BF16),
        scratch_shapes=[
            pltpu.VMEM((lat_total, 128), F32),
            pltpu.VMEM((degrees + 8, 128), F32),
            pltpu.VMEM((128 * block_rows, 128), F32),
        ],
        compiler_params=params(),
        name="analysis",
    )(firsts, arrived, basis)


def synthesis_body(degrees, low, count, block_rows, first_ref, in_ref, basis_ref, out_ref, *refs):
    held_ref, rows_ref, lats_ref = refs
    k = pl.program_id(0)
    first = first_ref[low + k]
    owners, lat_rows = out_ref.shape[0], out_ref.shape[2]

    @pl.when(k == 0)
    def _():
        held_ref[...] = in_ref[...].astype(F32).reshape(held_ref.shape)
        rows_ref[...] = jnp.zeros_like(rows_ref)

    for tile, start in enumerate(degree_starts(degrees, 8, block_rows, count)):
        rows_ref[8 * tile : 8 * tile + 8, :] = held_ref[pl.ds(start + k, 8, stride=block_rows), :]
    table = rows_ref[...]
    size = degrees + 8
    leading = pltpu.roll(table, lax.rem(size - first, size), 0)
    trailing = pltpu.roll(table, 1, 0)
    row = lax.broadcasted_iota(jnp.int32, (size, 128), 0)
    is_first = lax.broadcasted_iota(jnp.int32, (size, 128), 1) < 64
    lines = jnp.where(
        row < degrees - first,
        jnp.where(is_first, leading, 0.0),
        jnp.where(is_first, 0.0, trailing),
    )
    lats_ref[...] = tn_dot(basis_ref[0], lines[: degrees + 1].astype(BF16))
    for owner in range(owners):
        out_ref[owner, 0] = lats_ref[owner * lat_rows : (owner + 1) * lat_rows, :].astype(BF16)


def synthesize(filtered, basis, firsts, chunk, owners, lat_rows):
    low, high = chunk
    count = high - low
    slots, rows, lat_total = basis.shape
    degrees = rows - 1
    block_rows = filtered.shape[1]
    return pl.pallas_call(
        functools.partial(synthesis_body, degrees, low, count, block_rows),
        grid=(count,),
        in_specs=[
            pl.BlockSpec(memory_space=pltpu.SMEM),
            pl.BlockSpec((128, block_rows, 128), lambda k: (0, 0, 0)),
            pl.BlockSpec((1, rows, lat_total), lambda k: (low + k, 0, 0)),
        ],
        out_specs=pl.BlockSpec((owners, 1, lat_rows, 128), lambda k: (0, k, 0, 0)),
        out_shape=jax.ShapeDtypeStruct((owners, count, lat_rows, 128), BF16),
        scratch_shapes=[
            pltpu.VMEM((128 * block_rows, 128), F32),
            pltpu.VMEM((degrees + 8, 128), F32),
            pltpu.VMEM((lat_total, 128), F32),
        ],
        compiler_params=params(),
        name="synthesis",
    )(firsts, filtered, basis)


def gather_channels(in_ref, rows_ref, block_rows):
    def step(owner, _):
        start = pl.multiple_of(owner * block_rows, 8)
        for half in range(2):
            tiles = [in_ref[owner * 8 + 4 * half + a].astype(F32) for a in range(4)]
            for hj, tile in enumerate(swap_groups(tiles)):
                rows_ref[hj, pl.ds(start, block_rows), 128 * half : 128 * half + 128] = tile
        return 0

    lax.fori_loop(0, in_ref.shape[0] // 8, step, 0)


def row_degrees(block_rows, count, total):
    row = lax.broadcasted_iota(jnp.int32, (total // block_rows, block_rows, 256), 1)
    row = row.reshape(total, 256)
    return (row >= count).astype(jnp.int32) + (row >= 2 * count).astype(jnp.int32)


def filter_body(count, block_rows, in_ref, weight_ref, out_ref, degree_ref, rows_ref):
    gather_channels(in_ref, rows_ref, block_rows)
    total = rows_ref.shape[1]
    which = row_degrees(block_rows, count, total)
    weights = [weight_ref[:, s].reshape(256, 256) for s in range(3)]
    for hj in range(4):
        table = rows_ref[hj].astype(BF16)
        degree_ref[hj] = table
        kept = nt_dot(table, weights[0])
        kept = jnp.where(which == 1, nt_dot(table, weights[1]), kept)
        rows_ref[hj] = jnp.where(which == 2, nt_dot(table, weights[2]), kept)

    def step(owner, _):
        start = pl.multiple_of(owner * block_rows, 8)
        for half in range(2):
            tiles = [
                rows_ref[hj, pl.ds(start, block_rows), 128 * half : 128 * half + 128]
                for hj in range(4)
            ]
            for a, tile in enumerate(swap_groups(tiles)):
                out_ref[owner * 8 + 4 * half + a] = tile.astype(BF16)
        return 0

    lax.fori_loop(0, out_ref.shape[0] // 8, step, 0)


def spectral_filter(received, weights, count):
    devices, block_rows, _ = received.shape
    total = devices // 8 * block_rows
    return pl.pallas_call(
        functools.partial(filter_body, count, block_rows),
        out_shape=[
            jax.ShapeDtypeStruct(received.shape, BF16),
            jax.ShapeDtypeStruct((4, total, 256), BF16),
        ],
        scratch_shapes=[pltpu.VMEM((4, total, 256), F32)],
        compiler_params=params(),
        name="spectral_filter",
    )(received, weights)


def grad_body(counts, *refs):
    parts = len(counts)
    in_refs, degree_refs = refs[:parts], refs[parts : 2 * parts]
    out_ref = refs[2 * parts]
    scratch = refs[2 * parts + 1 :]
    sums = [None] * 3
    for count, in_ref, degree_ref, rows_ref in zip(counts, in_refs, degree_refs, scratch):
        block_rows = in_ref.shape[1]
        gather_channels(in_ref, rows_ref, block_rows)
        total = rows_ref.shape[1]
        which = row_degrees(block_rows, count, total)
        for hj in range(4):
            grad = rows_ref[hj]
            for s in range(3):
                term = tn_dot(jnp.where(which == s, grad, 0.0).astype(BF16), degree_ref[hj])
                sums[s] = term if sums[s] is None else sums[s] + term
    for s in range(3):
        out_ref[:, s] = sums[s].astype(BF16).reshape(8, GROUP, 256)


def filter_grad(received, by_degree, counts):
    return pl.pallas_call(
        functools.partial(grad_body, counts),
        out_shape=jax.ShapeDtypeStruct((8, 3, GROUP, 256), BF16),
        scratch_shapes=[pltpu.VMEM(table.shape, F32) for table in by_degree],
        compiler_params=params(),
        name="filter_grad",
    )(*received, *by_degree)


def exchange(array, axis):
    return lax.all_to_all(array, axis, split_axis=0, concat_axis=0, tiled=True)


def on_device(grid_in, lat_weights, legendre_basis, pair_list, filter_weights, cotangent):
    owners = lax.axis_size("lat")
    chans = lax.axis_size("chan")
    owner_index = lax.axis_index("lat")
    slots, rows, _ = legendre_basis.shape
    degrees = rows - 1
    _, lat_rows, chan_rows, lon_count = grid_in.shape
    grid, cotangent = grid_in[0], cotangent[0]
    firsts = lax.dynamic_slice_in_dim(pair_list, owner_index * slots, slots)
    scale = jnp.repeat(lat_weights, GROUP).reshape(1, -1)
    degrees_here = degrees // owners
    weights = lax.dynamic_slice_in_dim(filter_weights, owner_index * degrees_here, degrees_here, 0)
    weights = weights.reshape(degrees_here // chans, chans, chan_rows, -1).swapaxes(0, 1)
    weights = exchange(weights, "chan")
    table = longitude_table(degrees, lon_count, False)
    inverse_table = longitude_table(degrees, lon_count, True)

    everyone = ("lat", "chan")
    sent = forward_transform(grid, scale, pair_list, table, owners, slots)
    by_degree = []
    returned = []
    for part, chunk in zip(sent, CHUNKS):
        count = chunk[1] - chunk[0]
        coefficients = analysis(exchange(part, "lat"), legendre_basis, firsts, chunk)
        filtered, kept = spectral_filter(exchange(coefficients, everyone), weights, count)
        by_degree.append(kept)
        lines = synthesize(
            exchange(filtered, everyone), legendre_basis, firsts, chunk, owners, lat_rows
        )
        returned.append(exchange(lines, "lat"))
    block_out, *grads = middle_transform(
        returned, grid, cotangent, pair_list, inverse_table, owners, slots
    )
    received = []
    for part, chunk in zip(grads, CHUNKS):
        coefficients = analysis(exchange(part, "lat"), legendre_basis, firsts, chunk)
        received.append(exchange(coefficients, everyone))
    counts = tuple(high - low for low, high in CHUNKS)
    weight_grad = exchange(filter_grad(received, by_degree, counts), "chan")
    weight_grad = weight_grad.swapaxes(0, 1).reshape(degrees_here, chan_rows, -1).astype(F32)
    return (block_out[None], weight_grad)


def solution(mesh):
    in_specs = (
        P(None, "lat", "chan", None),
        P("lat"),
        P("lat", None, None),
        P(),
        P(None, "chan", None),
        P(None, "lat", "chan", None),
    )
    out_specs = (P(None, "lat", "chan", None), P("lat", "chan", None))
    return jax.shard_map(
        on_device, mesh=mesh, in_specs=in_specs, out_specs=out_specs, check_vma=False
    )
```

time: 644 us -> 321 us (0.50); the launches traced: 633 us -> 319 us
  local copies, waits for them, and re-layouts: 236 us -> 4.75 us
  waiting for transfers between devices: 183 us -> 33.7 us
  blocking collectives: 34.6 us -> 167 us
  matrix products: 131 us -> 0 us
  Pallas kernels: 0 us -> 100 us
  other arithmetic: 19.1 us -> 0.07 us
  between operations: 14.9 us -> 0.68 us
    all_to_all x1 -> x6, blocking collectives: 34.6 us -> 167 us  [exchange(): return lax.all_to_all(array, axis, split_axis=0, concat_axis=0, tiled=True)]
    dot_general x11 -> x0, matrix products: 131 us -> none  [the longest x2 34.5 us: to_spectrum(): jnp.einsum('btcn,gkwin->gktwibc', values, high_part, preferred_element_ty...]
    pallas_call x0 -> x7, Pallas kernels: none -> 100 us  [the longest x1 32.6 us: middle_transform(): pl.pallas_call(functools.partial(middle_body, pairs, slots), grid=(pl.cdi...]
    reduce_scatter x1 -> x0, waiting for transfers between devices: 71.4 us -> none  [on_device(): lax.psum_scatter(jnp.einsum('kwlibo,kwlibc->loc', degree_grad, by_degree,...]
    another operation x10 -> x1, local copies, waits for them, and re-layouts: 58.4 us -> 0.68 us  [on_device(): scale = jnp.repeat(lat_weights, GROUP).reshape(1, -1)]
    gather x5 -> x0, local copies, waits for them, and re-layouts: 52.5 us -> none  [the longest x4 40.3 us: lower_part(): return lax.dynamic_slice_in_dim(padded, degrees - offset, degrees, 0)]
    all_gather x1 -> x0, waiting for transfers between devices: 38.9 us -> none  [on_device(): all_coeffs = lax.all_gather(coefficients, 'chan', axis=4, tiled=True)]
    all_to_all x2, waiting for transfers between devices: 72.3 us -> 33.7 us  [exchange(): return lax.all_to_all(array, axis, split_axis=0, concat_axis=0, tiled=True)]
  transfers between devices with their start and end apart: 4 -> 2, of which waited for: 4 -> 1; matrix products, arithmetic and copies ran while one was open for 1% -> 1% of each run, Pallas kernels for 0% -> 4%
where the time goes in v1:
time: 321 us; the launch traced here: 319 us
  blocking collectives  167 us (52%)
  Pallas kernels  100 us (31%)
  waiting for transfers between devices  33.7 us (10%)
  starting transfers between devices  12.4 us (4%)
  local copies, waits for them, and re-layouts  4.75 us (1%)
    all_to_all x6, blocking collectives, exchange(): return lax.all_to_all(array, axis, split_axis=0, concat_axis=0, tiled=True)  167 us
    all_to_all x2, waiting for transfers between devices, exchange(): return lax.all_to_all(array, axis, split_axis=0, concat_axis=0, tiled=True)  33.7 us
    pallas_call x1, Pallas kernels, middle_transform(): pl.pallas_call(functools.partial(middle_body, pairs, slots), grid=(pl.cdi...  32.6 us
    pallas_call x2, Pallas kernels, analysis(): pl.pallas_call(functools.partial(analysis_body, degrees, low, count, bloc...  23.4 us
    pallas_call x1, Pallas kernels, forward_transform(): pl.pallas_call(functools.partial(forward_body, pairs, slots), grid=(pl.cd...  17.5 us
    all_to_all x2, starting transfers between devices, exchange(): return lax.all_to_all(array, axis, split_axis=0, concat_axis=0, tiled=True)  12.4 us
    pallas_call x1, Pallas kernels, synthesize(): pl.pallas_call(functools.partial(synthesis_body, degrees, low, count, blo...  12.4 us
    pallas_call x1, Pallas kernels, spectral_filter(): pl.pallas_call(functools.partial(filter_body, count, block_rows), out_sha...  8.26 us
  transfers between devices with their start and end apart: 2, of which 1 were waited for; matrix products, arithmetic and copies ran while one was open for 1% of the time, Pallas kernels for 4%

profile of v1, /device:TPU:0, one launch (start us, length us, event | category | flops | bytes accessed | tf_op | source)
XLA Modules:
  0.0 319.3 jit_solution(813012214122468565)
XLA Ops:
  0.6 0.7 broadcast_in_dim.6
  1.4 0.7 reshape_reshape.3.scale_ref
  2.0 17.5 %forward_transform.1 = bf16[16,12,45,128]{3,2,1,0:T(8,128)(2,1)} custom-call(s32[192]{0:T(256)} %pair_ref.3, bf16[45,32,1440]{2,1,0:T(8,128)(2,1)} %bitcast.10, f32[1,1440]{1,0:T(1,128)} %reshape_reshape.3.scale_ref, bf16[768,1440]{1,0:T(8,128)(2,1)} %constant.26.table_ref), custom_call_target="tpu_custom_call" | custom-call | tf_op jit(solution)/shard_map/forward_transform/pallas_call | solution.py:129
  19.5 8.1 %all-to-all-start = ((bf16[16,12,45,128]{3,2,1,0:T(8,128)(2,1)}), bf16[16,12,45,128]{3,2,1,0:T(8,128)(2,1)S(1)}, u32[]{:S(2)}, u32[]{:S(2)}) async-start(bf16[16,12,45,128]{3,2,1,0:T(8,128)(2,1)} %forward_transform.1), calls=%async_computation | async-start | bytes 4718592 | tf_op jit(solution)/shard_map/all_to_all | solution.py:423
  27.7 0.0 copy-start.2
  27.7 1.0 constant_dynamic-slice_fusion
  28.7 0.8 copy.13
  29.5 33.7 %all-to-all-done.in_ref = bf16[16,12,45,128]{3,2,1,0:T(8,128)(2,1)S(1)} async-done(((bf16[16,12,45,128]{3,2,1,0:T(8,128)(2,1)}), bf16[16,12,45,128]{3,2,1,0:T(8,128)(2,1)S(1)}, u32[]{:S(2)}, u32[]{:S(2)}) %all-to-all-start) | async-done | bytes 2211872 | tf_op jit(solution)/shard_map/all_to_all | solution.py:423
  63.2 0.0 copy-start
  63.2 4.3 %all-to-all-start.2 = ((bf16[8,3,32,256]{3,2,1,0:T(8,128)(2,1)}), bf16[8,3,32,256]{3,2,1,0:T(8,128)(2,1)S(1)}, u32[]{:S(2)}, u32[]{:S(2)}) async-start(bf16[8,3,32,256]{3,2,1,0:T(8,128)(2,1)} %bitcast.9), calls=%async_computation.2 | async-start | bytes 786432 | tf_op jit(solution)/shard_map/all_to_all | solution.py:423
  67.5 0.0 copy-done.2
  67.5 0.6 dynamic_slice.6.first_ref
  68.1 0.0 copy-done
  68.1 11.7 %analysis.2 = bf16[128,40,128]{2,1,0:T(8,128)(2,1)} custom-call(s32[12]{0:T(128)} %dynamic_slice.6.first_ref, bf16[16,12,45,128]{3,2,1,0:T(8,128)(2,1)} %copy-done, bf16[12,385,720]{2,1,0:T(8,128)(2,1)} %basis_ref.5), custom_call_target="tpu_custom_call" | custom-call | tf_op jit(solution)/shard_map/analysis/pallas_call | solution.py:258
  79.8 0.0 all-to-all-done.2.weight_ref
  79.8 0.0 copy-start.1
  79.8 29.4 %all_to_all.40.in_ref = bf16[128,40,128]{2,1,0:T(8,128)(2,1)} all-to-all(bf16[128,40,128]{2,1,0:T(8,128)(2,1)} %analysis.2), channel_id=1, replica_groups=mesh['lat'=16,'chan'=8] {'lat','chan'}, dimensions={0} | all-to-all | bytes 2621440 | tf_op jit(solution)/shard_map/all_to_all | solution.py:423
  109.2 0.0 copy-done.1
  109.2 8.3 %spectral_filter.1 = (bf16[128,40,128]{2,1,0:T(8,128)(2,1)}, bf16[4,640,256]{2,1,0:T(8,128)(2,1)}) custom-call(bf16[128,40,128]{2,1,0:T(8,128)(2,1)} %all_to_all.40.in_ref, bf16[8,3,32,256]{3,2,1,0:T(8,128)(2,1)} %copy-done.1), custom_call_target="tpu_custom_call" | custom-call | tf_op jit(solution)/shard_map/spectral_filter/pallas_call | solution.py:380
  117.5 27.5 %all_to_all.41.in_ref = bf16[128,40,128]{2,1,0:T(8,128)(2,1)} all-to-all(bf16[128,40,128]{2,1,0:T(8,128)(2,1)} %get-tuple-element.6), channel_id=1, replica_groups=mesh['lat'=16,'chan'=8] {'lat','chan'}, dimensions={0} | all-to-all | bytes 2621440 | tf_op jit(solution)/shard_map/all_to_all | solution.py:423
  145.0 12.4 %synthesis.1 = bf16[16,12,45,128]{3,2,1,0:T(8,128)(2,1)} custom-call(s32[12]{0:T(128)} %dynamic_slice.6.first_ref, bf16[128,40,128]{2,1,0:T(8,128)(2,1)} %all_to_all.41.in_ref, bf16[12,385,720]{2,1,0:T(8,128)(2,1)} %basis_ref.5), custom_call_target="tpu_custom_call" | custom-call | tf_op jit(solution)/shard_map/synthesis/pallas_call | solution.py:313
  157.3 35.7 %all_to_all.42.refs_0_ = bf16[16,12,45,128]{3,2,1,0:T(8,128)(2,1)} all-to-all(bf16[16,12,45,128]{3,2,1,0:T(8,128)(2,1)} %synthesis.1), channel_id=1, replica_groups=mesh['lat'=16,'chan'=8] {'lat'}, dimensions={0} | all-to-all | bytes 4423680 | tf_op jit(solution)/shard_map/all_to_all | solution.py:423
  193.1 32.6 %middle_transform.1 = (bf16[45,32,1440]{2,1,0:T(8,128)(2,1)}, bf16[16,12,45,128]{3,2,1,0:T(8,128)(2,1)}) custom-call(s32[192]{0:T(256)} %pair_ref.3, bf16[16,12,45,128]{3,2,1,0:T(8,128)(2,1)} %all_to_all.42.refs_0_, bf16[45,32,1440]{2,1,0:T(8,128)(2,1)} %bitcast.11, bf16[45,32,1440]{2,1,0:T(8,128)(2,1)} %bitcast.12, bf16[768,1440]{1,0:T(8,128)(2,1)} %constant.27.refs_3_), custom_call_target="tpu_custom_call" | custom-call | tf_op jit(solution)/shard_map/middle_transform/pallas_call | solution.py:190
  225.7 35.0 %all_to_all.43.in_ref = bf16[16,12,45,128]{3,2,1,0:T(8,128)(2,1)} all-to-all(bf16[16,12,45,128]{3,2,1,0:T(8,128)(2,1)} %get-tuple-element.8), channel_id=1, replica_groups=mesh['lat'=16,'chan'=8] {'lat'}, dimensions={0} | all-to-all | bytes 4423680 | tf_op jit(solution)/shard_map/all_to_all | solution.py:423
  260.7 11.7 %analysis.3 = bf16[128,40,128]{2,1,0:T(8,128)(2,1)} custom-call(s32[12]{0:T(128)} %dynamic_slice.6.first_ref, bf16[16,12,45,128]{3,2,1,0:T(8,128)(2,1)} %all_to_all.43.in_ref, bf16[12,385,720]{2,1,0:T(8,128)(2,1)} %basis_ref.5), custom_call_target="tpu_custom_call" | custom-call | tf_op jit(solution)/shard_map/analysis/pallas_call | solution.py:258
  272.5 27.5 %all_to_all.44.refs_0_ = bf16[128,40,128]{2,1,0:T(8,128)(2,1)} all-to-all(bf16[128,40,128]{2,1,0:T(8,128)(2,1)} %analysis.3), channel_id=1, replica_groups=mesh['lat'=16,'chan'=8] {'lat','chan'}, dimensions={0} | all-to-all | bytes 2621440 | tf_op jit(solution)/shard_map/all_to_all | solution.py:423
  300.0 6.0 %filter_grad.1 = bf16[8,3,32,256]{3,2,1,0:T(8,128)(2,1)} custom-call(bf16[128,40,128]{2,1,0:T(8,128)(2,1)} %all_to_all.44.refs_0_, bf16[4,640,256]{2,1,0:T(8,128)(2,1)} %get-tuple-element.9.refs_1_), custom_call_target="tpu_custom_call" | custom-call | tf_op jit(solution)/shard_map/filter_grad/pallas_call | solution.py:413
  306.0 12.3 %all_to_all.45 = bf16[8,3,32,256]{3,2,1,0:T(8,128)(2,1)S(1)} all-to-all(bf16[8,3,32,256]{3,2,1,0:T(8,128)(2,1)} %filter_grad.1), channel_id=1, replica_groups=mesh['lat'=16,'chan'=8] {'chan'}, dimensions={0} | all-to-all | bytes 786432 | tf_op jit(solution)/shard_map/all_to_all | solution.py:423
  318.3 0.1 convert_bitcast_fusion
  318.4 0.9 copy.11
Async XLA Ops:
  19.5 43.6 %all-to-all-start = ((bf16[16,12,45,128]{3,2,1,0:T(8,128)(2,1)}), bf16[16,12,45,128]{3,2,1,0:T(8,128)(2,1)S(1)}, u32[]{:S(2)}, u32[]{:S(2)}) async-start(bf16[16,12,45,128]{3,2,1,0:T(8,128)(2,1)} %forward_transform.1), calls=%async_computation | async-start | bytes 4718592 | tf_op jit(solution)/shard_map/all_to_all | solution.py:423
  27.7 39.8 %copy-start.2 = (s32[192]{0:T(256)S(1)}, s32[192]{0:T(256)}, u32[]{:S(2)}) copy-start(s32[192]{0:T(256)} %pair_ref.3) | copy-start | bytes 2308
  63.2 4.9 %copy-start = (bf16[16,12,45,128]{3,2,1,0:T(8,128)(2,1)}, bf16[16,12,45,128]{3,2,1,0:T(8,128)(2,1)S(1)}, u32[]{:S(2)}) copy-start(bf16[16,12,45,128]{3,2,1,0:T(8,128)(2,1)S(1)} %all-to-all-done.in_ref) | copy-start | bytes 6635524
  63.2 16.6 %all-to-all-start.2 = ((bf16[8,3,32,256]{3,2,1,0:T(8,128)(2,1)}), bf16[8,3,32,256]{3,2,1,0:T(8,128)(2,1)S(1)}, u32[]{:S(2)}, u32[]{:S(2)}) async-start(bf16[8,3,32,256]{3,2,1,0:T(8,128)(2,1)} %bitcast.9), calls=%async_computation.2 | async-start | bytes 786432 | tf_op jit(solution)/shard_map/all_to_all | solution.py:423
  79.8 29.4 %copy-start.1 = (bf16[8,3,32,256]{3,2,1,0:T(8,128)(2,1)}, bf16[8,3,32,256]{3,2,1,0:T(8,128)(2,1)S(1)}, u32[]{:S(2)}) copy-start(bf16[8,3,32,256]{3,2,1,0:T(8,128)(2,1)S(1)} %all-to-all-done.2.weight_ref) | copy-start | bytes 1179652

commit v2 on v0

v2 whole, which is shorter than its diff:
```python
import functools
import math

import jax
import jax.numpy as jnp
import numpy as np
from jax import lax
from jax.experimental import pallas as pl
from jax.experimental.pallas import tpu as pltpu
from jax.sharding import PartitionSpec as P

F32 = jnp.float32
BF16 = jnp.bfloat16
GROUP = 32
T_STEP = 16
T_PART = 8
S_STEP = 4


def params(mib=56):
    return pltpu.CompilerParams(vmem_limit_bytes=mib << 20)


def cost(microseconds):
    return pl.CostEstimate(
        flops=int(microseconds * 1e9), bytes_accessed=1 << 20, transcendentals=0
    )


def round_up(value, unit):
    return -(-value // unit) * unit


def longitude_table(degrees, lon_count, doubled):
    first = np.arange(degrees // 2)
    orders = np.stack([first, degrees - 1 - first])
    phases = orders[:, :, None] * np.arange(lon_count) % lon_count
    angles = phases * (2.0 * math.pi / lon_count)
    table = np.stack([np.cos(angles), -np.sin(angles)], axis=1) / math.sqrt(lon_count)
    if doubled:
        table = table * np.where(orders == 0, 1.0, 2.0)[:, None, :, None]
    return jnp.asarray(table.reshape(2 * degrees, lon_count).astype(np.float32)).astype(BF16)


def swap_groups(tiles):
    lane = lax.broadcasted_iota(jnp.int32, tiles[0].shape, 1)
    low, even = lane < 64, lane // GROUP % 2 == 0
    t0, t1, t2, t3 = tiles
    a0 = jnp.where(low, t0, pltpu.roll(t2, 64, 1))
    a1 = jnp.where(low, t1, pltpu.roll(t3, 64, 1))
    a2 = jnp.where(low, pltpu.roll(t0, 64, 1), t2)
    a3 = jnp.where(low, pltpu.roll(t1, 64, 1), t3)
    return [
        jnp.where(even, a0, pltpu.roll(a1, 32, 1)),
        jnp.where(even, pltpu.roll(a0, 96, 1), a1),
        jnp.where(even, a2, pltpu.roll(a3, 32, 1)),
        jnp.where(even, pltpu.roll(a2, 96, 1), a3),
    ]


P_BLOCK = 32
PAD = 1


def by_latitude(rows_ref, stacked_ref, pairs, part, weight_of):
    for start in range(0, pairs, P_BLOCK):
        for q in range(T_PART // 4):
            lanes = slice(128 * q, 128 * q + 128)
            tiles = [
                rows_ref[part, wi * pairs + start : wi * pairs + start + P_BLOCK, lanes]
                for wi in range(4)
            ]
            for s, tile in enumerate(swap_groups(tiles)):
                t = part * T_PART + 4 * q + s
                row = t * (pairs + PAD) + start
                stacked_ref[row : row + P_BLOCK, :] = tile if weight_of is None else tile * weight_of[t]


def by_order(stacked_ref, rows_ref, pairs, q):
    for start in range(0, pairs, P_BLOCK):
        tiles = []
        for s in range(4):
            row = (4 * q + s) * (pairs + PAD) + start
            tiles.append(stacked_ref[row : row + P_BLOCK, :])
        for wi, tile in enumerate(swap_groups(tiles)):
            row = wi * pairs + start
            rows_ref[row : row + P_BLOCK, 128 * q : 128 * q + 128] = tile.astype(BF16)


def send_slots(pair_ref, stacked_ref, out_ref, pairs, slots):
    def step(owner, _):
        for k in range(slots):
            order = pair_ref[owner * slots + k]
            tile = stacked_ref[pl.ds(order, T_STEP, stride=pairs + PAD), :]
            out_ref[owner, k] = tile.astype(BF16)
        return 0

    lax.fori_loop(0, pairs // slots, step, 0)


def nt_dot(a, b):
    return lax.dot_general(a, b, (((1,), (1,)), ((), ())), preferred_element_type=F32)


def tn_dot(a, b):
    return lax.dot_general(a, b, (((0,), (0,)), ((), ())), preferred_element_type=F32)


def forward_body(pairs, slots, lat_rows, pair_ref, weight_ref, grid_ref, table_ref, out_ref, *refs):
    rows_ref, stacked_ref = refs
    start = pl.program_id(0) * T_STEP
    weight_of = [weight_ref[jnp.minimum(start + t, lat_rows - 1)] for t in range(T_STEP)]
    for part in range(T_STEP // T_PART):
        fields = grid_ref[part * T_PART : (part + 1) * T_PART].reshape(T_PART * GROUP, -1)
        rows_ref[part] = nt_dot(table_ref[...], fields)
        by_latitude(rows_ref, stacked_ref, pairs, part, weight_of)
    send_slots(pair_ref, stacked_ref, out_ref, pairs, slots)


def slot_spec(owners, slots):
    return pl.BlockSpec((owners, slots, T_STEP, 128), lambda t: (0, 0, t, 0))


def turn_scratch(pairs):
    return [
        pltpu.VMEM((T_STEP // T_PART, 4 * pairs, T_PART * GROUP), F32),
        pltpu.VMEM((T_STEP * (pairs + PAD), 128), F32),
    ]


def forward_transform(grid, weights, pair_list, table, owners, slots):
    lat_rows, _, lon_count = grid.shape
    pairs = owners * slots
    return pl.pallas_call(
        functools.partial(forward_body, pairs, slots, lat_rows),
        grid=(pl.cdiv(lat_rows, T_STEP),),
        in_specs=[
            pl.BlockSpec(memory_space=pltpu.SMEM),
            pl.BlockSpec(memory_space=pltpu.SMEM),
            pl.BlockSpec((T_STEP, GROUP, lon_count), lambda t: (t, 0, 0)),
            pl.BlockSpec((4 * pairs, lon_count), lambda t: (0, 0)),
        ],
        out_specs=slot_spec(owners, slots),
        out_shape=jax.ShapeDtypeStruct((owners, slots, lat_rows, 128), BF16),
        scratch_shapes=turn_scratch(pairs),
        compiler_params=params(),
        cost_estimate=cost(12),
        name="forward_transform",
    )(pair_list, weights, grid, table)


def middle_body(pairs, slots, pair_ref, in_ref, grid_ref, cot_ref, table_ref, *refs):
    field_ref, out_ref, rows_ref, stacked_ref, lines_ref, grad_ref = refs

    def step(owner, _):
        for k in range(slots):
            order = pair_ref[owner * slots + k]
            tile = in_ref[owner, k].astype(F32)
            stacked_ref[pl.ds(order, T_STEP, stride=pairs + PAD), :] = tile
        return 0

    lax.fori_loop(0, pairs // slots, step, 0)
    root = math.sqrt(2.0 / math.pi)
    for q in range(T_STEP // 4):
        by_order(stacked_ref, lines_ref, pairs, q)
        rows = slice(128 * q, 128 * q + 128)
        lats = slice(4 * q, 4 * q + 4)
        x = tn_dot(lines_ref[:, rows], table_ref[...])
        square = x * x
        th = jnp.tanh(x * (root + (root * 0.044715) * square))
        half = 0.5 + 0.5 * th
        gate = x * half
        slope = half + gate * (1.0 - th) * (root + (3.0 * root * 0.044715) * square)
        grid = grid_ref[lats].reshape(128, -1).astype(F32)
        field_ref[lats] = (grid + gate).astype(BF16).reshape(4, GROUP, -1)
        cot = cot_ref[lats].reshape(128, -1).astype(F32)
        grad_ref[rows, :] = (cot * slope).astype(BF16)
    for part in range(T_STEP // T_PART):
        grads = grad_ref[part * T_PART * GROUP : (part + 1) * T_PART * GROUP, :]
        rows_ref[part] = nt_dot(table_ref[...], grads)
        by_latitude(rows_ref, stacked_ref, pairs, part, None)
    send_slots(pair_ref, stacked_ref, out_ref, pairs, slots)


def middle_transform(returned, grid, cotangent, pair_list, table, owners, slots):
    lat_rows, _, lon_count = grid.shape
    pairs = owners * slots
    field_spec = pl.BlockSpec((T_STEP, GROUP, lon_count), lambda t: (t, 0, 0))
    return pl.pallas_call(
        functools.partial(middle_body, pairs, slots),
        grid=(pl.cdiv(lat_rows, T_STEP),),
        in_specs=[
            pl.BlockSpec(memory_space=pltpu.SMEM),
            slot_spec(owners, slots),
            field_spec,
            field_spec,
            pl.BlockSpec((4 * pairs, lon_count), lambda t: (0, 0)),
        ],
        out_specs=[field_spec, slot_spec(owners, slots)],
        out_shape=[
            jax.ShapeDtypeStruct(grid.shape, BF16),
            jax.ShapeDtypeStruct((owners, slots, lat_rows, 128), BF16),
        ],
        scratch_shapes=turn_scratch(pairs)
        + [
            pltpu.VMEM((4 * pairs, T_STEP * GROUP), BF16),
            pltpu.VMEM((T_STEP * GROUP, lon_count), BF16),
        ],
        compiler_params=params(),
        cost_estimate=cost(25),
        name="middle_transform",
    )(pair_list, returned, grid, cotangent, table)


def owned_tiles(degrees, chans, owners):
    return [divmod(tile, degrees // chans // owners) for tile in range(degrees // chans)]


def analysis_body(spread, firsts_ref, in_ref, basis_ref, out_ref, lats_ref, rows_ref, *refs):
    step = pl.program_id(0)
    owners, steps, lat_rows, _ = in_ref.shape
    degrees = basis_ref.shape[1] - 1
    degree = lax.broadcasted_iota(jnp.int32, (degrees, 128), 0)
    is_first = lax.broadcasted_iota(jnp.int32, (degrees, 128), 1) < 64

    if spread:
        sent_ref = refs[0]

        @pl.when(step == 0)
        def _():
            sent_ref[...] = jnp.zeros_like(sent_ref)

    for k in range(steps):
        for owner in range(owners):
            lats_ref[k, owner * lat_rows : (owner + 1) * lat_rows, :] = in_ref[owner, k].astype(F32)
        rows_ref[k, degrees + 1 :, :] = jnp.zeros((7, 128), F32)
    for k in range(steps):
        spectrum = lats_ref[k].astype(BF16)
        rows_ref[k, : degrees + 1, :] = jnp.dot(
            basis_ref[k], spectrum, preferred_element_type=F32
        )
    for k in range(steps):
        slot = step * steps + k
        first = firsts_ref[slot]
        leading = pltpu.roll(rows_ref[k], first, 0)[:degrees]
        trailing = rows_ref[k, 1 : degrees + 1, :]
        smallest = jnp.where(is_first, first, degrees - 1 - first)
        table = jnp.where(degree >= smallest, jnp.where(is_first, leading, trailing), 0.0)
        if spread:
            block_rows = out_ref.shape[1]
            for tile, (i, s) in enumerate(owned_tiles(degrees, 8, owners)):
                row = 8 * i * block_rows + 3 * slot + s
                sent_ref[pl.ds(row, 8, stride=block_rows), :] = table[8 * tile : 8 * tile + 8]
        else:
            part = degrees // owners
            for owner in range(owners):
                out_ref[owner, k] = table[part * owner : part * (owner + 1)].astype(BF16)

    if spread:

        @pl.when(step == pl.num_programs(0) - 1)
        def _():
            out_ref[...] = sent_ref[...].astype(BF16).reshape(out_ref.shape)


def analysis(arrived, basis, firsts, spread):
    owners, slots, lat_rows, _ = arrived.shape
    _, rows, lat_total = basis.shape
    degrees = rows - 1
    scratch = [
        pltpu.VMEM((S_STEP, lat_total, 128), F32),
        pltpu.VMEM((S_STEP, degrees + 8, 128), F32),
    ]
    if spread:
        block_rows = round_up(3 * slots, 8)
        shape = (owners * 8, block_rows, 128)
        out_spec = pl.BlockSpec(shape, lambda k: (0, 0, 0))
        scratch.append(pltpu.VMEM((owners * 8 * block_rows, 128), F32))
    else:
        part = degrees // owners
        shape = (owners, slots, part, 128)
        out_spec = pl.BlockSpec((owners, S_STEP, part, 128), lambda k: (0, k, 0, 0))
    return pl.pallas_call(
        functools.partial(analysis_body, spread),
        grid=(slots // S_STEP,),
        in_specs=[
            pl.BlockSpec(memory_space=pltpu.SMEM),
            pl.BlockSpec((owners, S_STEP, lat_rows, 128), lambda k: (0, k, 0, 0)),
            pl.BlockSpec((S_STEP, rows, lat_total), lambda k: (k, 0, 0)),
        ],
        out_specs=out_spec,
        out_shape=jax.ShapeDtypeStruct(shape, BF16),
        scratch_shapes=scratch,
        compiler_params=params(),
        cost_estimate=cost(6),
        name="analysis",
    )(firsts, arrived, basis)


def synthesis_body(firsts_ref, in_ref, basis_ref, out_ref, held_ref, rows_ref, lats_ref):
    step = pl.program_id(0)
    owners, steps, lat_rows, _ = out_ref.shape
    degrees = basis_ref.shape[1] - 1
    block_rows = in_ref.shape[1]
    size = degrees + 8
    row = lax.broadcasted_iota(jnp.int32, (size, 128), 0)
    is_first = lax.broadcasted_iota(jnp.int32, (size, 128), 1) < 64

    @pl.when(step == 0)
    def _():
        held_ref[...] = in_ref[...].astype(F32).reshape(held_ref.shape)
        rows_ref[...] = jnp.zeros_like(rows_ref)

    for k in range(steps):
        slot = step * steps + k
        for tile, (i, s) in enumerate(owned_tiles(degrees, 8, owners)):
            start = 8 * i * block_rows + 3 * slot + s
            rows_ref[k, 8 * tile : 8 * tile + 8, :] = held_ref[pl.ds(start, 8, stride=block_rows), :]
    for k in range(steps):
        first = firsts_ref[step * steps + k]
        table = rows_ref[k]
        leading = pltpu.roll(table, lax.rem(size - first, size), 0)
        trailing = pltpu.roll(table, 1, 0)
        lines = jnp.where(
            row < degrees - first,
            jnp.where(is_first, leading, 0.0),
            jnp.where(is_first, 0.0, trailing),
        )
        lats_ref[k] = tn_dot(basis_ref[k], lines[: degrees + 1].astype(BF16))
    for k in range(steps):
        for owner in range(owners):
            out_ref[owner, k] = lats_ref[k, owner * lat_rows : (owner + 1) * lat_rows, :].astype(BF16)


def synthesize(filtered, basis, firsts, owners, lat_rows):
    slots, rows, lat_total = basis.shape
    degrees = rows - 1
    devices, block_rows, _ = filtered.shape
    return pl.pallas_call(
        synthesis_body,
        grid=(slots // S_STEP,),
        in_specs=[
            pl.BlockSpec(memory_space=pltpu.SMEM),
            pl.BlockSpec((devices, block_rows, 128), lambda k: (0, 0, 0)),
            pl.BlockSpec((S_STEP, rows, lat_total), lambda k: (k, 0, 0)),
        ],
        out_specs=pl.BlockSpec((owners, S_STEP, lat_rows, 128), lambda k: (0, k, 0, 0)),
        out_shape=jax.ShapeDtypeStruct((owners, slots, lat_rows, 128), BF16),
        scratch_shapes=[
            pltpu.VMEM((devices * block_rows, 128), F32),
            pltpu.VMEM((S_STEP, degrees + 8, 128), F32),
            pltpu.VMEM((S_STEP, lat_total, 128), F32),
        ],
        compiler_params=params(),
        cost_estimate=cost(7),
        name="synthesis",
    )(firsts, filtered, basis)


HELD = 48
OWNER_UNROLL = 2


def filter_body(slots, me_ref, in_ref, weight_ref, out_ref, degree_ref, rows_ref, kept_ref, tight_ref):
    devices, block_rows, _ = in_ref.shape
    owners = devices // 8

    def gather(owner, _):
        start = pl.multiple_of(owner * HELD, 8)
        for half in range(2):
            lanes = slice(128 * half, 128 * half + 128)
            tiles = [in_ref[owner * 8 + 4 * half + a].astype(F32) for a in range(4)]
            for hj, tile in enumerate(swap_groups(tiles)):
                rows_ref[hj, half, pl.ds(start, block_rows), :] = tile
                rows_ref[hj, half, pl.ds(start + block_rows, HELD - block_rows), :] = jnp.zeros(
                    (HELD - block_rows, 128), F32
                )
        return 0

    lax.fori_loop(0, owners, gather, 0, unroll=OWNER_UNROLL)
    per_owner = HELD // 3
    for s in range(3):
        weights = weight_ref[:, s, 0].reshape(256, 256)
        for hj in range(4):
            table = [
                rows_ref[hj, half, pl.ds(s, owners * per_owner, stride=3), :] for half in range(2)
            ]
            for half in range(2):
                for i in range(owners):
                    row = (hj * owners + i) * slots
                    tight_ref[row : row + slots, 128 * half : 128 * half + 128] = table[half][
                        per_owner * i : per_owner * i + slots
                    ]
            whole = jnp.concatenate([half.astype(BF16) for half in table], axis=1)
            product = nt_dot(whole, weights)
            for half in range(2):
                kept_ref[hj, half, pl.ds(s, owners * per_owner, stride=3), :] = product[
                    :, 128 * half : 128 * half + 128
                ]
        degree_ref[s] = tight_ref[...].astype(BF16)

    def scatter(owner, _):
        start = pl.multiple_of(owner * HELD, 8)
        for half in range(2):
            tiles = [kept_ref[hj, half, pl.ds(start, block_rows), :] for hj in range(4)]
            for a, tile in enumerate(swap_groups(tiles)):
                out_ref[owner * 8 + 4 * half + a] = tile.astype(BF16)
        return 0

    lax.fori_loop(0, owners, scatter, 0, unroll=OWNER_UNROLL)


def spectral_filter(received, weights, me, slots):
    devices, block_rows, _ = received.shape
    owners = devices // 8
    whole = lambda shape: pl.BlockSpec(shape, lambda n, me_ref: (0,) * len(shape))
    degree_shape = (3, 4 * owners * slots, 256)
    return pl.pallas_call(
        functools.partial(filter_body, slots),
        grid_spec=pltpu.PrefetchScalarGridSpec(
            num_scalar_prefetch=1,
            grid=(1,),
            in_specs=[
                whole(received.shape),
                pl.BlockSpec((8, 3, 1, GROUP, 256), lambda n, me_ref: (0, 0, me_ref[0], 0, 0)),
            ],
            out_specs=[whole(received.shape), whole(degree_shape)],
            scratch_shapes=[
                pltpu.VMEM((4, 2, owners * HELD, 128), F32),
                pltpu.VMEM((4, 2, owners * HELD, 128), F32),
                pltpu.VMEM((4 * owners * slots, 256), F32),
            ],
        ),
        out_shape=[
            jax.ShapeDtypeStruct(received.shape, BF16),
            jax.ShapeDtypeStruct(degree_shape, BF16),
        ],
        compiler_params=params(),
        cost_estimate=cost(6),
        name="spectral_filter",
    )(me, received, weights)


def grad_body(in_ref, degree_ref, out_ref, rows_ref):
    step = pl.program_id(0)
    owners, slots, part, _ = in_ref.shape

    @pl.when(step == 0)
    def _():
        rows_ref[...] = in_ref[...].astype(F32).reshape(rows_ref.shape)

    group = lax.broadcasted_iota(jnp.int32, (owners * slots, 128), 1) // GROUP
    for j in range(8):
        grad = rows_ref[pl.ds(8 * step + j, owners * slots, stride=part), :]
        spread = [jnp.where(group == hj, grad, 0.0).astype(BF16) for hj in range(4)]
        sums = tn_dot(jnp.concatenate(spread, axis=0), degree_ref[j, 0])
        total = sums[:GROUP] + sums[GROUP : 2 * GROUP]
        out_ref[j] = total + (sums[2 * GROUP : 3 * GROUP] + sums[3 * GROUP :])


def filter_grad(received, by_degree):
    owners, slots, part, _ = received.shape
    chans, steps, rows, _ = by_degree.shape
    return pl.pallas_call(
        grad_body,
        grid=(steps,),
        in_specs=[
            pl.BlockSpec(received.shape, lambda s: (0, 0, 0, 0)),
            pl.BlockSpec((chans, 1, rows, 256), lambda s: (0, s, 0, 0)),
        ],
        out_specs=pl.BlockSpec((chans, GROUP, 256), lambda s: (s, 0, 0)),
        out_shape=jax.ShapeDtypeStruct((part, GROUP, 256), F32),
        scratch_shapes=[pltpu.VMEM((owners * slots * part, 128), F32)],
        compiler_params=params(),
        cost_estimate=cost(6),
        name="filter_grad",
    )(received, by_degree)


def exchange(array, axis):
    return lax.all_to_all(array, axis, split_axis=0, concat_axis=0, tiled=True)


def on_device(grid_in, lat_weights, legendre_basis, pair_list, filter_weights, cotangent):
    owners = lax.axis_size("lat")
    chans = lax.axis_size("chan")
    owner_index = lax.axis_index("lat")
    slots, rows, _ = legendre_basis.shape
    degrees = rows - 1
    _, lat_rows, chan_rows, lon_count = grid_in.shape
    grid, cotangent = grid_in[0], cotangent[0]
    firsts = lax.dynamic_slice_in_dim(pair_list, owner_index * slots, slots)
    me = lax.axis_index("chan").reshape(1).astype(jnp.int32)
    part = degrees // owners
    table = longitude_table(degrees, lon_count, False)
    inverse_table = longitude_table(degrees, lon_count, True)

    everyone = ("lat", "chan")
    spectrum = forward_transform(grid, lat_weights, pair_list, table, owners, slots)
    spectrum, filter_weights = lax.optimization_barrier((spectrum, filter_weights))
    weights = lax.dynamic_slice_in_dim(filter_weights, owner_index * part, part, 0)
    weights = lax.all_gather(weights, "chan")
    weights = weights.reshape(chans, part // chans, chans, chan_rows, -1)
    coefficients = analysis(exchange(spectrum, "lat"), legendre_basis, firsts, True)
    filtered, by_degree = spectral_filter(exchange(coefficients, everyone), weights, me, slots)
    filtered, by_degree = lax.optimization_barrier((exchange(filtered, everyone), by_degree))
    by_degree = lax.all_gather(by_degree, "chan")
    lines = synthesize(filtered, legendre_basis, firsts, owners, lat_rows)
    block_out, grads = middle_transform(
        exchange(lines, "lat"), grid, cotangent, pair_list, inverse_table, owners, slots
    )
    grads = analysis(exchange(grads, "lat"), legendre_basis, firsts, False)
    weight_grad = filter_grad(exchange(grads, "lat"), by_degree)
    return (block_out[None], weight_grad)


def solution(mesh):
    in_specs = (
        P(None, "lat", "chan", None),
        P("lat"),
        P("lat", None, None),
        P(),
        P(None, "chan", None),
        P(None, "lat", "chan", None),
    )
    out_specs = (P(None, "lat", "chan", None), P("lat", "chan", None))
    return jax.shard_map(
        on_device, mesh=mesh, in_specs=in_specs, out_specs=out_specs, check_vma=False
    )
```

time: 644 us -> 278 us (0.43); the launches traced: 633 us -> 277 us
  local copies, waits for them, and re-layouts: 236 us -> 4.83 us
  matrix products: 131 us -> 0 us
  waiting for transfers between devices: 183 us -> 56.8 us
  blocking collectives: 34.6 us -> 119 us
  Pallas kernels: 0 us -> 67.2 us
  other arithmetic: 19.1 us -> 0 us
    dot_general x11 -> x0, matrix products: 131 us -> none  [the longest x2 34.5 us: to_spectrum(): jnp.einsum('btcn,gkwin->gktwibc', values, high_part, preferred_element_ty...]
    all_to_all x1 -> x4, blocking collectives: 34.6 us -> 119 us  [exchange(): return lax.all_to_all(array, axis, split_axis=0, concat_axis=0, tiled=True)]
    reduce_scatter x1 -> x0, waiting for transfers between devices: 71.4 us -> none  [on_device(): lax.psum_scatter(jnp.einsum('kwlibo,kwlibc->loc', degree_grad, by_degree,...]
    pallas_call x0 -> x7, Pallas kernels: none -> 67.2 us  [the longest x1 21 us: middle_transform(): pl.pallas_call(functools.partial(middle_body, pairs, slots), grid=(pl.cdi...]
    another operation x10 -> x0, local copies, waits for them, and re-layouts: 58.4 us -> none
    gather x5 -> x0, local copies, waits for them, and re-layouts: 52.5 us -> none  [the longest x4 40.3 us: lower_part(): return lax.dynamic_slice_in_dim(padded, degrees - offset, degrees, 0)]
    all_gather x1 -> x2, waiting for transfers between devices: 38.9 us -> 0.01 us  [the longest x1 0.01 us: on_device(): weights = lax.all_gather(weights, 'chan')]
    concatenate x3 -> x0, local copies, waits for them, and re-layouts: 30.6 us -> none  [the longest x2 24.8 us: lower_part(): jnp.concatenate([jnp.zeros((degrees,) + block_rows.shape[1:], block_rows....]
  transfers between devices with their start and end apart: 4 -> 4, of which waited for: 4 -> 2; matrix products, arithmetic and copies ran while one was open for 1% -> 0% of each run, Pallas kernels for 0% -> 16%
where the time goes in v2:
time: 278 us; the launch traced here: 277 us
  blocking collectives  119 us (43%)
  Pallas kernels  67.2 us (24%)
  waiting for transfers between devices  56.8 us (20%)
  starting transfers between devices  15.1 us (5%)
  between operations  14.1 us (5%)
  local copies, waits for them, and re-layouts  4.83 us (2%)
    all_to_all x4, blocking collectives, exchange(): return lax.all_to_all(array, axis, split_axis=0, concat_axis=0, tiled=True)  119 us
    all_to_all x2, waiting for transfers between devices, exchange(): return lax.all_to_all(array, axis, split_axis=0, concat_axis=0, tiled=True)  56.8 us
    pallas_call x1, Pallas kernels, middle_transform(): pl.pallas_call(functools.partial(middle_body, pairs, slots), grid=(pl.cdi...  21 us
    all_to_all x2, starting transfers between devices, exchange(): return lax.all_to_all(array, axis, split_axis=0, concat_axis=0, tiled=True)  15 us
    pallas_call x2, Pallas kernels, analysis(): pl.pallas_call(functools.partial(analysis_body, spread), grid=(slots // S...  14.7 us
    pallas_call x1, Pallas kernels, forward_transform(): pl.pallas_call(functools.partial(forward_body, pairs, slots, lat_rows), g...  10.2 us
    pallas_call x1, Pallas kernels, synthesize(): pl.pallas_call(synthesis_body, grid=(slots // S_STEP,), in_specs=[pl.Bloc...  8.29 us
    pallas_call x1, Pallas kernels, filter_grad(): pl.pallas_call(grad_body, grid=(steps,), in_specs=[pl.BlockSpec(received....  6.51 us
  transfers between devices with their start and end apart: 4, of which 2 were waited for; matrix products, arithmetic and copies ran while one was open for 0% of the time, Pallas kernels for 16%

profile of v2, /device:TPU:0, one launch (start us, length us, event | category | flops | bytes accessed | tf_op | source)
XLA Modules:
  0.0 277.0 jit_solution(1051695423460106911)
XLA Ops:
  7.2 0.0 all-gather.5.cloned.1.call-start
  7.2 10.2 %forward_transform.1 = bf16[16,12,45,128]{3,2,1,0:T(8,128)(2,1)} custom-call(s32[192]{0:T(256)} %pair_ref.3, f32[45]{0:T(128)} %weight_ref.1, bf16[45,32,1440]{2,1,0:T(8,128)(2,1)} %bitcast.7, bf16[768,1440]{1,0:T(8,128)(2,1)} %constant.29.table_ref), custom_call_target="tpu_custom_call" | custom-call | flops 12000000000 | bytes 1048576 | tf_op jit(solution)/shard_map/forward_transform/pallas_call | solution.py:134
  17.4 1.8 constant_dynamic-slice_fusion
  19.2 0.0 all-gather.5.cloned.1.call-update
  19.2 0.0 copy-start.2
  19.2 8.1 %all-to-all-start = ((bf16[16,12,45,128]{3,2,1,0:T(8,128)(2,1)}), bf16[16,12,45,128]{3,2,1,0:T(8,128)(2,1)S(1)}, u32[]{:S(2)}, u32[]{:S(2)}) async-start(bf16[16,12,45,128]{3,2,1,0:T(8,128)(2,1)} %forward_transform.1), calls=%async_computation | async-start | bytes 4718592 | tf_op jit(solution)/shard_map/all_to_all | solution.py:481
  27.4 0.0 copy-done.2
  27.4 0.6 dynamic_slice.6.firsts_ref
  28.0 34.9 %all-to-all-done.in_ref = bf16[16,12,45,128]{3,2,1,0:T(8,128)(2,1)S(1)} async-done(((bf16[16,12,45,128]{3,2,1,0:T(8,128)(2,1)}), bf16[16,12,45,128]{3,2,1,0:T(8,128)(2,1)S(1)}, u32[]{:S(2)}, u32[]{:S(2)}) %all-to-all-start) | async-done | bytes 2211872 | tf_op jit(solution)/shard_map/all_to_all | solution.py:481
  62.9 0.0 copy-start
  62.9 1.4 copy-done
  64.3 7.7 %analysis.2 = bf16[128,40,128]{2,1,0:T(8,128)(2,1)} custom-call(s32[12]{0:T(128)} %dynamic_slice.6.firsts_ref, bf16[16,12,45,128]{3,2,1,0:T(8,128)(2,1)} %copy-done, bf16[12,385,720]{2,1,0:T(8,128)(2,1)} %basis_ref.5), custom_call_target="tpu_custom_call" | custom-call | flops 6000000000 | bytes 1048576 | tf_op jit(solution)/shard_map/analysis/pallas_call | solution.py:283
  71.9 6.8 %all-to-all-start.1 = ((bf16[128,40,128]{2,1,0:T(8,128)(2,1)}), bf16[128,40,128]{2,1,0:T(8,128)(2,1)S(1)}, u32[]{:S(2)}, u32[]{:S(2)}) async-start(bf16[128,40,128]{2,1,0:T(8,128)(2,1)} %analysis.2), calls=%async_computation.1 | async-start | bytes 2621440 | tf_op jit(solution)/shard_map/all_to_all | solution.py:481
  78.8 0.0 all-gather.7.cloned.1.call-start
  78.8 21.9 %all-to-all-done.1.in_ref = bf16[128,40,128]{2,1,0:T(8,128)(2,1)S(1)} async-done(((bf16[128,40,128]{2,1,0:T(8,128)(2,1)}), bf16[128,40,128]{2,1,0:T(8,128)(2,1)S(1)}, u32[]{:S(2)}, u32[]{:S(2)}) %all-to-all-start.1) | async-done | bytes 1310752 | tf_op jit(solution)/shard_map/all_to_all | solution.py:481
  100.7 0.0 copy-start.1
  100.7 0.0 all-gather.5.cloned.1.call-done
  100.7 1.1 copy-done.1
  101.8 6.4 %spectral_filter.1 = (bf16[128,40,128]{2,1,0:T(8,128)(2,1)}, bf16[3,768,256]{2,1,0:T(8,128)(2,1)}) custom-call(s32[1]{0:T(128)} %bitcast.me_ref, bf16[128,40,128]{2,1,0:T(8,128)(2,1)} %copy-done.1, bf16[8,3,8,32,256]{4,3,2,1,0:T(8,128)(2,1)} %bitcast.10), custom_call_target="tpu_custom_call" | custom-call | flops 6000000000 | bytes 1048576 | tf_op jit(solution)/shard_map/spectral_filter/pallas_call | solution.py:418
  108.2 27.5 %all_to_all.30.in_ref = bf16[128,40,128]{2,1,0:T(8,128)(2,1)} all-to-all(bf16[128,40,128]{2,1,0:T(8,128)(2,1)} %get-tuple-element.12), channel_id=1, replica_groups=mesh['lat'=16,'chan'=8] {'lat','chan'}, dimensions={0} | all-to-all | bytes 2621440 | tf_op jit(solution)/shard_map/all_to_all | solution.py:481
  135.8 0.0 all-gather.7.cloned.1.call-update
  135.8 8.3 %synthesis.1 = bf16[16,12,45,128]{3,2,1,0:T(8,128)(2,1)} custom-call(s32[12]{0:T(128)} %dynamic_slice.6.firsts_ref, bf16[128,40,128]{2,1,0:T(8,128)(2,1)} %all_to_all.30.in_ref, bf16[12,385,720]{2,1,0:T(8,128)(2,1)} %basis_ref.5), custom_call_target="tpu_custom_call" | custom-call | flops 7000000000 | bytes 1048576 | tf_op jit(solution)/shard_map/synthesis/pallas_call | solution.py:339
  144.1 35.7 %all_to_all.31.in_ref = bf16[16,12,45,128]{3,2,1,0:T(8,128)(2,1)} all-to-all(bf16[16,12,45,128]{3,2,1,0:T(8,128)(2,1)} %synthesis.1), channel_id=1, replica_groups=mesh['lat'=16,'chan'=8] {'lat'}, dimensions={0} | all-to-all | bytes 4423680 | tf_op jit(solution)/shard_map/all_to_all | solution.py:481
  179.8 21.0 %middle_transform.1 = (bf16[45,32,1440]{2,1,0:T(8,128)(2,1)}, bf16[16,12,45,128]{3,2,1,0:T(8,128)(2,1)}) custom-call(s32[192]{0:T(256)} %pair_ref.3, bf16[16,12,45,128]{3,2,1,0:T(8,128)(2,1)} %all_to_all.31.in_ref, bf16[45,32,1440]{2,1,0:T(8,128)(2,1)} %bitcast.8, bf16[45,32,1440]{2,1,0:T(8,128)(2,1)} %bitcast.9, bf16[768,1440]{1,0:T(8,128)(2,1)} %constant.30.table_ref), custom_call_target="tpu_custom_call" | custom-call | flops 24999999488 | bytes 1048576 | tf_op jit(solution)/shard_map/middle_transform/pallas_call | solution.py:189
  200.8 34.9 %all_to_all.32.in_ref = bf16[16,12,45,128]{3,2,1,0:T(8,128)(2,1)} all-to-all(bf16[16,12,45,128]{3,2,1,0:T(8,128)(2,1)} %get-tuple-element.16), channel_id=1, replica_groups=mesh['lat'=16,'chan'=8] {'lat'}, dimensions={0} | all-to-all | bytes 4423680 | tf_op jit(solution)/shard_map/all_to_all | solution.py:481
  235.7 7.1 %analysis.3 = bf16[16,12,24,128]{3,2,1,0:T(8,128)(2,1)} custom-call(s32[12]{0:T(128)} %dynamic_slice.6.firsts_ref, bf16[16,12,45,128]{3,2,1,0:T(8,128)(2,1)} %all_to_all.32.in_ref, bf16[12,385,720]{2,1,0:T(8,128)(2,1)} %basis_ref.5), custom_call_target="tpu_custom_call" | custom-call | flops 6000000000 | bytes 1048576 | tf_op jit(solution)/shard_map/analysis/pallas_call | solution.py:283
  242.7 21.0 %all_to_all.33.in_ref = bf16[16,12,24,128]{3,2,1,0:T(8,128)(2,1)} all-to-all(bf16[16,12,24,128]{3,2,1,0:T(8,128)(2,1)} %analysis.3), channel_id=1, replica_groups=mesh['lat'=16,'chan'=8] {'lat'}, dimensions={0} | all-to-all | bytes 2359296 | tf_op jit(solution)/shard_map/all_to_all | solution.py:481
  263.7 0.0 all-gather.7.cloned.1.call-done
  263.7 6.5 %filter_grad.1 = f32[24,32,256]{2,1,0:T(8,128)} custom-call(bf16[16,12,24,128]{3,2,1,0:T(8,128)(2,1)} %all_to_all.33.in_ref, bf16[8,3,768,256]{3,2,1,0:T(8,128)(2,1)} %bitcast.6), custom_call_target="tpu_custom_call" | custom-call | flops 6000000000 | bytes 1048576 | tf_op jit(solution)/shard_map/filter_grad/pallas_call | solution.py:464
Async XLA Ops:
  7.2 93.6 %all-gather.5.cloned.1.call-start = ((), (), s32[]{:S(2)}) async-start(), calls=%async_computation.6 | async-start | bytes 3538944 | tf_op jit(solution)/shard_map/all_gather | solution.py:502
  19.2 8.2 %copy-start.2 = (s32[192]{0:T(256)S(1)}, s32[192]{0:T(256)}, u32[]{:S(2)}) copy-start(s32[192]{0:T(256)} %pair_ref.3) | copy-start | bytes 2308
  19.2 43.7 %all-to-all-start = ((bf16[16,12,45,128]{3,2,1,0:T(8,128)(2,1)}), bf16[16,12,45,128]{3,2,1,0:T(8,128)(2,1)S(1)}, u32[]{:S(2)}, u32[]{:S(2)}) async-start(bf16[16,12,45,128]{3,2,1,0:T(8,128)(2,1)} %forward_transform.1), calls=%async_computation | async-start | bytes 4718592 | tf_op jit(solution)/shard_map/all_to_all | solution.py:481
  62.9 1.4 copy-start
  71.9 28.8 %all-to-all-start.1 = ((bf16[128,40,128]{2,1,0:T(8,128)(2,1)}), bf16[128,40,128]{2,1,0:T(8,128)(2,1)S(1)}, u32[]{:S(2)}, u32[]{:S(2)}) async-start(bf16[128,40,128]{2,1,0:T(8,128)(2,1)} %analysis.2), calls=%async_computation.1 | async-start | bytes 2621440 | tf_op jit(solution)/shard_map/all_to_all | solution.py:481
  78.8 184.9 %all-gather.7.cloned.1.call-start = ((), (), s32[]{:S(2)}) async-start(), calls=%async_computation.7 | async-start | bytes 10616832 | tf_op jit(solution)/shard_map/all_gather | solution.py:507
  100.7 1.1 copy-start.1
Sparse Core Ops, SparseCore 0:
  19.3 30.1 all-gather.4
  135.9 49.8 all-gather.6

commit v3 on v2

--- a/solution.py
+++ b/solution.py
@@ -17,7 +17,7 @@
 S_STEP = 4
 
 
-def params(mib=56):
+def params(mib):
     return pltpu.CompilerParams(vmem_limit_bytes=mib << 20)
 
 
@@ -106,9 +106,14 @@
     return lax.dot_general(a, b, (((0,), (0,)), ((), ())), preferred_element_type=F32)
 
 
-def forward_body(pairs, slots, lat_rows, pair_ref, weight_ref, grid_ref, table_ref, out_ref, *refs):
-    rows_ref, stacked_ref = refs
+def forward_body(pairs, slots, lat_rows, owner_ref, pair_ref, weight_ref, *refs):
+    grid_ref, table_ref, filter_ref, out_ref, part_ref, rows_ref, stacked_ref = refs
     start = pl.program_id(0) * T_STEP
+
+    @pl.when(start == 0)
+    def _():
+        part_ref[...] = filter_ref[...]
+
     weight_of = [weight_ref[jnp.minimum(start + t, lat_rows - 1)] for t in range(T_STEP)]
     for part in range(T_STEP // T_PART):
         fields = grid_ref[part * T_PART : (part + 1) * T_PART].reshape(T_PART * GROUP, -1)
@@ -128,28 +133,39 @@
     ]
 
 
-def forward_transform(grid, weights, pair_list, table, owners, slots):
+def forward_transform(grid, weights, pair_list, table, filters, owner, owners, slots):
     lat_rows, _, lon_count = grid.shape
     pairs = owners * slots
+    part_shape = (filters.shape[0] // owners,) + filters.shape[1:]
     return pl.pallas_call(
         functools.partial(forward_body, pairs, slots, lat_rows),
-        grid=(pl.cdiv(lat_rows, T_STEP),),
-        in_specs=[
-            pl.BlockSpec(memory_space=pltpu.SMEM),
-            pl.BlockSpec(memory_space=pltpu.SMEM),
-            pl.BlockSpec((T_STEP, GROUP, lon_count), lambda t: (t, 0, 0)),
-            pl.BlockSpec((4 * pairs, lon_count), lambda t: (0, 0)),
-        ],
-        out_specs=slot_spec(owners, slots),
-        out_shape=jax.ShapeDtypeStruct((owners, slots, lat_rows, 128), BF16),
-        scratch_shapes=turn_scratch(pairs),
-        compiler_params=params(),
+        grid_spec=pltpu.PrefetchScalarGridSpec(
+            num_scalar_prefetch=1,
+            grid=(pl.cdiv(lat_rows, T_STEP),),
+            in_specs=[
+                pl.BlockSpec(memory_space=pltpu.SMEM),
+                pl.BlockSpec(memory_space=pltpu.SMEM),
+                pl.BlockSpec((T_STEP, GROUP, lon_count), lambda t, owner_ref: (t, 0, 0)),
+                pl.BlockSpec((4 * pairs, lon_count), lambda t, owner_ref: (0, 0)),
+                pl.BlockSpec(part_shape, lambda t, owner_ref: (owner_ref[0], 0, 0)),
+            ],
+            out_specs=[
+                pl.BlockSpec((owners, slots, T_STEP, 128), lambda t, owner_ref: (0, 0, t, 0)),
+                pl.BlockSpec(part_shape, lambda t, owner_ref: (0, 0, 0)),
+            ],
+            scratch_shapes=turn_scratch(pairs),
+        ),
+        out_shape=[
+            jax.ShapeDtypeStruct((owners, slots, lat_rows, 128), BF16),
+            jax.ShapeDtypeStruct(part_shape, BF16),
+        ],
+        compiler_params=params(56),
         cost_estimate=cost(12),
         name="forward_transform",
-    )(pair_list, weights, grid, table)
-
-
-def middle_body(pairs, slots, pair_ref, in_ref, grid_ref, cot_ref, table_ref, *refs):
+    )(owner, pair_list, weights, grid, table, filters)
+
+
+def middle_body(pairs, slots, pair_ref, in_ref, cot_ref, table_ref, *refs):
     field_ref, out_ref, rows_ref, stacked_ref, lines_ref, grad_ref = refs
 
     def step(owner, _):
@@ -171,8 +187,7 @@
         half = 0.5 + 0.5 * th
         gate = x * half
         slope = half + gate * (1.0 - th) * (root + (3.0 * root * 0.044715) * square)
-        grid = grid_ref[lats].reshape(128, -1).astype(F32)
-        field_ref[lats] = (grid + gate).astype(BF16).reshape(4, GROUP, -1)
+        field_ref[lats] = gate.astype(BF16).reshape(4, GROUP, -1)
         cot = cot_ref[lats].reshape(128, -1).astype(F32)
         grad_ref[rows, :] = (cot * slope).astype(BF16)
     for part in range(T_STEP // T_PART):
@@ -182,8 +197,8 @@
     send_slots(pair_ref, stacked_ref, out_ref, pairs, slots)
 
 
-def middle_transform(returned, grid, cotangent, pair_list, table, owners, slots):
-    lat_rows, _, lon_count = grid.shape
+def middle_transform(returned, cotangent, pair_list, table, owners, slots):
+    lat_rows, _, lon_count = cotangent.shape
     pairs = owners * slots
     field_spec = pl.BlockSpec((T_STEP, GROUP, lon_count), lambda t: (t, 0, 0))
     return pl.pallas_call(
@@ -193,12 +208,11 @@
             pl.BlockSpec(memory_space=pltpu.SMEM),
             slot_spec(owners, slots),
             field_spec,
-            field_spec,
             pl.BlockSpec((4 * pairs, lon_count), lambda t: (0, 0)),
         ],
         out_specs=[field_spec, slot_spec(owners, slots)],
         out_shape=[
-            jax.ShapeDtypeStruct(grid.shape, BF16),
+            jax.ShapeDtypeStruct(cotangent.shape, BF16),
             jax.ShapeDtypeStruct((owners, slots, lat_rows, 128), BF16),
         ],
         scratch_shapes=turn_scratch(pairs)
@@ -206,17 +220,17 @@
             pltpu.VMEM((4 * pairs, T_STEP * GROUP), BF16),
             pltpu.VMEM((T_STEP * GROUP, lon_count), BF16),
         ],
-        compiler_params=params(),
+        compiler_params=params(46),
         cost_estimate=cost(25),
         name="middle_transform",
-    )(pair_list, returned, grid, cotangent, table)
+    )(pair_list, returned, cotangent, table)
 
 
 def owned_tiles(degrees, chans, owners):
     return [divmod(tile, degrees // chans // owners) for tile in range(degrees // chans)]
 
 
-def analysis_body(spread, firsts_ref, in_ref, basis_ref, out_ref, lats_ref, rows_ref, *refs):
+def analysis_body(spread, owner_ref, pair_ref, in_ref, basis_ref, out_ref, lats_ref, rows_ref, *refs):
     step = pl.program_id(0)
     owners, steps, lat_rows, _ = in_ref.shape
     degrees = basis_ref.shape[1] - 1
@@ -241,7 +255,7 @@
         )
     for k in range(steps):
         slot = step * steps + k
-        first = firsts_ref[slot]
+        first = pair_ref[owner_ref[0] * pl.num_programs(0) * steps + slot]
         leading = pltpu.roll(rows_ref[k], first, 0)[:degrees]
         trailing = rows_ref[k, 1 : degrees + 1, :]
         smallest = jnp.where(is_first, first, degrees - 1 - first)
@@ -263,7 +277,7 @@
             out_ref[...] = sent_ref[...].astype(BF16).reshape(out_ref.shape)
 
 
-def analysis(arrived, basis, firsts, spread):
+def analysis(arrived, basis, places, spread):
     owners, slots, lat_rows, _ = arrived.shape
     _, rows, lat_total = basis.shape
     degrees = rows - 1
@@ -285,19 +299,20 @@
         grid=(slots // S_STEP,),
         in_specs=[
             pl.BlockSpec(memory_space=pltpu.SMEM),
+            pl.BlockSpec(memory_space=pltpu.SMEM),
             pl.BlockSpec((owners, S_STEP, lat_rows, 128), lambda k: (0, k, 0, 0)),
             pl.BlockSpec((S_STEP, rows, lat_total), lambda k: (k, 0, 0)),
         ],
         out_specs=out_spec,
         out_shape=jax.ShapeDtypeStruct(shape, BF16),
         scratch_shapes=scratch,
-        compiler_params=params(),
+        compiler_params=params(18),
         cost_estimate=cost(6),
         name="analysis",
-    )(firsts, arrived, basis)
-
-
-def synthesis_body(firsts_ref, in_ref, basis_ref, out_ref, held_ref, rows_ref, lats_ref):
+    )(*places, arrived, basis)
+
+
+def synthesis_body(owner_ref, pair_ref, in_ref, basis_ref, out_ref, held_ref, rows_ref, lats_ref):
     step = pl.program_id(0)
     owners, steps, lat_rows, _ = out_ref.shape
     degrees = basis_ref.shape[1] - 1
@@ -317,7 +332,7 @@
             start = 8 * i * block_rows + 3 * slot + s
             rows_ref[k, 8 * tile : 8 * tile + 8, :] = held_ref[pl.ds(start, 8, stride=block_rows), :]
     for k in range(steps):
-        first = firsts_ref[step * steps + k]
+        first = pair_ref[(owner_ref[0] * pl.num_programs(0) + step) * steps + k]
         table = rows_ref[k]
         leading = pltpu.roll(table, lax.rem(size - first, size), 0)
         trailing = pltpu.roll(table, 1, 0)
@@ -332,7 +347,7 @@
             out_ref[owner, k] = lats_ref[k, owner * lat_rows : (owner + 1) * lat_rows, :].astype(BF16)
 
 
-def synthesize(filtered, basis, firsts, owners, lat_rows):
+def synthesize(filtered, basis, places, owners, lat_rows):
     slots, rows, lat_total = basis.shape
     degrees = rows - 1
     devices, block_rows, _ = filtered.shape
@@ -341,6 +356,7 @@
         grid=(slots // S_STEP,),
         in_specs=[
             pl.BlockSpec(memory_space=pltpu.SMEM),
+            pl.BlockSpec(memory_space=pltpu.SMEM),
             pl.BlockSpec((devices, block_rows, 128), lambda k: (0, 0, 0)),
             pl.BlockSpec((S_STEP, rows, lat_total), lambda k: (k, 0, 0)),
         ],
@@ -351,10 +367,10 @@
             pltpu.VMEM((S_STEP, degrees + 8, 128), F32),
             pltpu.VMEM((S_STEP, lat_total, 128), F32),
         ],
-        compiler_params=params(),
+        compiler_params=params(18),
         cost_estimate=cost(7),
         name="synthesis",
-    )(firsts, filtered, basis)
+    )(*places, filtered, basis)
 
 
 HELD = 48
@@ -435,7 +451,7 @@
             jax.ShapeDtypeStruct(received.shape, BF16),
             jax.ShapeDtypeStruct(degree_shape, BF16),
         ],
-        compiler_params=params(),
+        compiler_params=params(22),
         cost_estimate=cost(6),
         name="spectral_filter",
     )(me, received, weights)
@@ -471,7 +487,7 @@
         out_specs=pl.BlockSpec((chans, GROUP, 256), lambda s: (s, 0, 0)),
         out_shape=jax.ShapeDtypeStruct((part, GROUP, 256), F32),
         scratch_shapes=[pltpu.VMEM((owners * slots * part, 128), F32)],
-        compiler_params=params(),
+        compiler_params=params(40),
         cost_estimate=cost(6),
         name="filter_grad",
     )(received, by_degree)
@@ -484,33 +500,33 @@
 def on_device(grid_in, lat_weights, legendre_basis, pair_list, filter_weights, cotangent):
     owners = lax.axis_size("lat")
     chans = lax.axis_size("chan")
-    owner_index = lax.axis_index("lat")
     slots, rows, _ = legendre_basis.shape
     degrees = rows - 1
     _, lat_rows, chan_rows, lon_count = grid_in.shape
     grid, cotangent = grid_in[0], cotangent[0]
-    firsts = lax.dynamic_slice_in_dim(pair_list, owner_index * slots, slots)
+    owner = lax.axis_index("lat").reshape(1).astype(jnp.int32)
     me = lax.axis_index("chan").reshape(1).astype(jnp.int32)
-    part = degrees // owners
+    places = (owner, pair_list)
     table = longitude_table(degrees, lon_count, False)
     inverse_table = longitude_table(degrees, lon_count, True)
 
     everyone = ("lat", "chan")
-    spectrum = forward_transform(grid, lat_weights, pair_list, table, owners, slots)
-    spectrum, filter_weights = lax.optimization_barrier((spectrum, filter_weights))
-    weights = lax.dynamic_slice_in_dim(filter_weights, owner_index * part, part, 0)
+    spectrum, weights = forward_transform(
+        grid, lat_weights, pair_list, table, filter_weights, owner, owners, slots
+    )
     weights = lax.all_gather(weights, "chan")
-    weights = weights.reshape(chans, part // chans, chans, chan_rows, -1)
-    coefficients = analysis(exchange(spectrum, "lat"), legendre_basis, firsts, True)
+    weights = weights.reshape(chans, degrees // owners // chans, chans, chan_rows, -1)
+    coefficients = analysis(exchange(spectrum, "lat"), legendre_basis, places, True)
     filtered, by_degree = spectral_filter(exchange(coefficients, everyone), weights, me, slots)
     filtered, by_degree = lax.optimization_barrier((exchange(filtered, everyone), by_degree))
     by_degree = lax.all_gather(by_degree, "chan")
-    lines = synthesize(filtered, legendre_basis, firsts, owners, lat_rows)
-    block_out, grads = middle_transform(
-        exchange(lines, "lat"), grid, cotangent, pair_list, inverse_table, owners, slots
+    lines = synthesize(filtered, legendre_basis, places, owners, lat_rows)
+    gate, grads = middle_transform(
+        exchange(lines, "lat"), cotangent, pair_list, inverse_table, owners, slots
     )
-    grads = analysis(exchange(grads, "lat"), legendre_basis, firsts, False)
+    grads = analysis(exchange(grads, "lat"), legendre_basis, places, False)
     weight_grad = filter_grad(exchange(grads, "lat"), by_degree)
+    block_out = (grid.astype(F32) + gate.astype(F32)).astype(BF16)
     return (block_out[None], weight_grad)
 
 

time: 278 us -> 262 us (0.942)
  waiting for transfers between devices: 56.8 us -> 31.9 us
  Pallas kernels: 67.2 us -> 53.2 us
  blocking collectives: 119 us -> 133 us
  other arithmetic: 0 us -> 7.56 us
  local copies, waits for them, and re-layouts: 4.83 us -> 11.7 us
  starting transfers between devices: 15.1 us -> 9.89 us
    all_to_all x2, waiting for transfers between devices: 56.8 us -> 31.8 us  [exchange(): return lax.all_to_all(array, axis, split_axis=0, concat_axis=0, tiled=True)]
    all_to_all x4, blocking collectives: 119 us -> 133 us  [exchange(): return lax.all_to_all(array, axis, split_axis=0, concat_axis=0, tiled=True)]
    unnamed x6 -> x16, local copies, waits for them, and re-layouts: 2.46 us -> 11.7 us
    broadcast_in_dim x0 -> x1, other arithmetic: none -> 7.56 us  [on_device(): return (block_out[None], weight_grad)]
    all_to_all x2, starting transfers between devices: 15 us -> 9.81 us  [exchange(): return lax.all_to_all(array, axis, split_axis=0, concat_axis=0, tiled=True)]
    pallas_call x2, Pallas kernels: 14.7 us -> 10.6 us  [analysis(): pl.pallas_call(functools.partial(analysis_body, spread), grid=(slots // S...]
    pallas_call x1, Pallas kernels: 6.51 us -> 3.46 us  [filter_grad(): pl.pallas_call(grad_body, grid=(steps,), in_specs=[pl.BlockSpec(received....]
    pallas_call x1, Pallas kernels: 8.29 us -> 5.37 us  [synthesize(): pl.pallas_call(synthesis_body, grid=(slots // S_STEP,), in_specs=[pl.Bloc...]
  transfers between devices with their start and end apart: 4 -> 4, of which waited for: 2 -> 2; matrix products, arithmetic and copies ran while one was open for 0% -> 3% of each run, Pallas kernels for 16% -> 13%
where the time goes in v3:
time: 262 us
  blocking collectives  133 us (51%)
  Pallas kernels  53.2 us (20%)
  waiting for transfers between devices  31.9 us (12%)
  between operations  14.1 us (5%)
  local copies, waits for them, and re-layouts  11.7 us (4%)
  starting transfers between devices  9.89 us (4%)
  other arithmetic  7.56 us (3%)
    all_to_all x4, blocking collectives, exchange(): return lax.all_to_all(array, axis, split_axis=0, concat_axis=0, tiled=True)  133 us
    all_to_all x2, waiting for transfers between devices, exchange(): return lax.all_to_all(array, axis, split_axis=0, concat_axis=0, tiled=True)  31.8 us
    pallas_call x1, Pallas kernels, middle_transform(): pl.pallas_call(functools.partial(middle_body, pairs, slots), grid=(pl.cdi...  18.7 us
    unnamed x16, local copies, waits for them, and re-layouts  11.7 us
    pallas_call x2, Pallas kernels, analysis(): pl.pallas_call(functools.partial(analysis_body, spread), grid=(slots // S...  10.6 us
    pallas_call x1, Pallas kernels, forward_transform(): pl.pallas_call(functools.partial(forward_body, pairs, slots, lat_rows), g...  10.4 us
    all_to_all x2, starting transfers between devices, exchange(): return lax.all_to_all(array, axis, split_axis=0, concat_axis=0, tiled=True)  9.81 us
    broadcast_in_dim x1, other arithmetic, on_device(): return (block_out[None], weight_grad)  7.56 us
  transfers between devices with their start and end apart: 4, of which 2 were waited for; matrix products, arithmetic and copies ran while one was open for 3% of the time, Pallas kernels for 13%

profile of v3, /device:TPU:0, one launch (start us, length us, event | category | flops | bytes accessed | tf_op | source)
XLA Modules:
  0.0 261.8 jit_solution(9865321807984962539)
XLA Ops:
  7.2 0.0 all-gather.5.cloned.1.call-start
  7.2 10.4 %forward_transform.1 = (bf16[16,12,45,128]{3,2,1,0:T(8,128)(2,1)}, bf16[24,32,256]{2,1,0:T(8,128)(2,1)}) custom-call(s32[1]{0:T(128)} %bitcast.1.owner_ref, s32[192]{0:T(256)} %pair_ref.9, f32[45]{0:T(128)} %weight_ref.1, bf16[45,32,1440]{2,1,0:T(8,128)(2,1)} %bitcast.13, bf16[768,1440]{1,0:T(8,128)(2,1)} %constant.19.refs_1_, bf16[384,32,256]{2,1,0:T(8,128)(2,1)} %refs_2_.1), custom_call_target="tpu_custom_call" | custom-call | flops 12000000000 | bytes 1048576 | tf_op jit(solution)/shard_map/forward_transform/pallas_call | solution.py:140
  17.6 0.0 all-gather.5.cloned.1.call-update
  17.6 0.0 copy-start.4
  17.7 39.3 %all_to_all.30.in_ref = bf16[16,12,45,128]{3,2,1,0:T(8,128)(2,1)S(1)} all-to-all(bf16[16,12,45,128]{3,2,1,0:T(8,128)(2,1)} %get-tuple-element.10), channel_id=1, replica_groups=mesh['lat'=16,'chan'=8] {'lat'}, dimensions={0} | all-to-all | bytes 4423680 | tf_op jit(solution)/shard_map/all_to_all | solution.py:497
  57.0 0.0 copy-done.4
  57.0 0.0 copy-start.1
  57.0 3.0 %copy-done.1 = bf16[12,385,720]{2,1,0:T(8,128)(2,1)S(1)} copy-done((bf16[12,385,720]{2,1,0:T(8,128)(2,1)S(1)}, bf16[12,385,720]{2,1,0:T(8,128)(2,1)}, u32[]{:S(2)}) %copy-start.1) | copy-done | bytes 6652824
  60.1 5.7 %analysis.2 = bf16[128,40,128]{2,1,0:T(8,128)(2,1)} custom-call(s32[1]{0:T(128)} %bitcast.1.owner_ref, s32[192]{0:T(256)S(1)} %copy-done.4, bf16[16,12,45,128]{3,2,1,0:T(8,128)(2,1)S(1)} %all_to_all.30.in_ref, bf16[12,385,720]{2,1,0:T(8,128)(2,1)S(1)} %copy-done.1), custom_call_target="tpu_custom_call" | custom-call | flops 6000000000 | bytes 1048576 | tf_op jit(solution)/shard_map/analysis/pallas_call | solution.py:297
  65.7 6.1 %all-to-all-start.1 = ((bf16[128,40,128]{2,1,0:T(8,128)(2,1)}), bf16[128,40,128]{2,1,0:T(8,128)(2,1)S(1)}, u32[]{:S(2)}, u32[]{:S(2)}) async-start(bf16[128,40,128]{2,1,0:T(8,128)(2,1)} %analysis.2), calls=%async_computation.1 | async-start | bytes 2621440 | tf_op jit(solution)/shard_map/all_to_all | solution.py:497
  71.9 0.0 all-gather.7.cloned.1.call-start
  71.9 21.9 %all-to-all-done.1.in_ref = bf16[128,40,128]{2,1,0:T(8,128)(2,1)S(1)} async-done(((bf16[128,40,128]{2,1,0:T(8,128)(2,1)}), bf16[128,40,128]{2,1,0:T(8,128)(2,1)S(1)}, u32[]{:S(2)}, u32[]{:S(2)}) %all-to-all-start.1) | async-done | bytes 1310752 | tf_op jit(solution)/shard_map/all_to_all | solution.py:497
  93.8 0.0 all-gather.5.cloned.1.call-done
  93.8 0.0 copy-start.3
  93.8 1.9 copy-done.3
  95.7 4.7 %spectral_filter.1 = (bf16[128,40,128]{2,1,0:T(8,128)(2,1)S(1)}, bf16[3,768,256]{2,1,0:T(8,128)(2,1)}) custom-call(s32[1]{0:T(128)} %bitcast.2.me_ref, bf16[128,40,128]{2,1,0:T(8,128)(2,1)S(1)} %all-to-all-done.1.in_ref, bf16[8,3,8,32,256]{4,3,2,1,0:T(8,128)(2,1)S(1)} %bitcast.12), custom_call_target="tpu_custom_call" | custom-call | flops 6000000000 | bytes 1048576 | tf_op jit(solution)/shard_map/spectral_filter/pallas_call | solution.py:434
  100.4 26.2 %all_to_all.31.in_ref = bf16[128,40,128]{2,1,0:T(8,128)(2,1)S(1)} all-to-all(bf16[128,40,128]{2,1,0:T(8,128)(2,1)S(1)} %get-tuple-element.12), channel_id=1, replica_groups=mesh['lat'=16,'chan'=8] {'lat','chan'}, dimensions={0} | all-to-all | bytes 2621440 | tf_op jit(solution)/shard_map/all_to_all | solution.py:497
  126.6 0.0 all-gather.7.cloned.1.call-update
  126.6 0.0 copy-start.2
  126.6 3.0 %copy-done.2 = bf16[12,385,720]{2,1,0:T(8,128)(2,1)S(1)} copy-done((bf16[12,385,720]{2,1,0:T(8,128)(2,1)S(1)}, bf16[12,385,720]{2,1,0:T(8,128)(2,1)}, u32[]{:S(2)}) %copy-start.2) | copy-done | bytes 6652824
  129.7 0.0 copy-start.5
  129.7 5.4 %synthesis.1 = bf16[16,12,45,128]{3,2,1,0:T(8,128)(2,1)S(1)} custom-call(s32[1]{0:T(128)} %bitcast.1.owner_ref, s32[192]{0:T(256)S(1)} %copy-done.4, bf16[128,40,128]{2,1,0:T(8,128)(2,1)S(1)} %all_to_all.31.in_ref, bf16[12,385,720]{2,1,0:T(8,128)(2,1)S(1)} %copy-done.2), custom_call_target="tpu_custom_call" | custom-call | flops 7000000000 | bytes 1048576 | tf_op jit(solution)/shard_map/synthesis/pallas_call | solution.py:354
  135.1 0.0 slice-start
  135.1 34.2 %all_to_all.32.in_ref = bf16[16,12,45,128]{3,2,1,0:T(8,128)(2,1)S(1)} all-to-all(bf16[16,12,45,128]{3,2,1,0:T(8,128)(2,1)S(1)} %synthesis.1), channel_id=1, replica_groups=mesh['lat'=16,'chan'=8] {'lat'}, dimensions={0} | all-to-all | bytes 4423680 | tf_op jit(solution)/shard_map/all_to_all | solution.py:497
  169.3 0.0 copy-done.5
  169.3 0.0 slice-start.1
  169.3 18.7 %middle_transform.1 = (bf16[45,32,1440]{2,1,0:T(8,128)(2,1)}, bf16[16,12,45,128]{3,2,1,0:T(8,128)(2,1)S(1)}) custom-call(s32[192]{0:T(256)S(1)} %copy-done.4, bf16[16,12,45,128]{3,2,1,0:T(8,128)(2,1)S(1)} %all_to_all.32.in_ref, bf16[45,32,1440]{2,1,0:T(8,128)(2,1)} %bitcast.14, bf16[768,1440]{1,0:T(8,128)(2,1)S(1)} %copy-done.5), custom_call_target="tpu_custom_call" | custom-call | flops 24999999488 | bytes 1048576 | tf_op jit(solution)/shard_map/middle_transform/pallas_call | solution.py:204
  188.0 33.7 %all_to_all.33.in_ref = bf16[16,12,45,128]{3,2,1,0:T(8,128)(2,1)S(1)} all-to-all(bf16[16,12,45,128]{3,2,1,0:T(8,128)(2,1)S(1)} %get-tuple-element.16), channel_id=1, replica_groups=mesh['lat'=16,'chan'=8] {'lat'}, dimensions={0} | all-to-all | bytes 4423680 | tf_op jit(solution)/shard_map/all_to_all | solution.py:497
  221.7 0.0 slice-done
  221.7 0.0 slice-done.1
  221.7 4.9 %analysis.3 = bf16[16,12,24,128]{3,2,1,0:T(8,128)(2,1)} custom-call(s32[1]{0:T(128)} %bitcast.1.owner_ref, s32[192]{0:T(256)S(1)} %copy-done.4, bf16[16,12,45,128]{3,2,1,0:T(8,128)(2,1)S(1)} %all_to_all.33.in_ref, bf16[12,385,720]{2,1,0:T(8,128)(2,1)S(1)} %bitcast.11), custom_call_target="tpu_custom_call" | custom-call | flops 6000000000 | bytes 1048576 | tf_op jit(solution)/shard_map/analysis/pallas_call | solution.py:297
  226.6 3.7 %all-to-all-start.5 = ((bf16[16,12,24,128]{3,2,1,0:T(8,128)(2,1)}), bf16[16,12,24,128]{3,2,1,0:T(8,128)(2,1)S(1)}, u32[]{:S(2)}, u32[]{:S(2)}) async-start(bf16[16,12,24,128]{3,2,1,0:T(8,128)(2,1)} %analysis.3), calls=%async_computation.5 | async-start | bytes 2359296 | tf_op jit(solution)/shard_map/all_to_all | solution.py:497
  230.3 7.6 %fusion = bf16[1,45,32,1440]{3,2,1,0:T(8,128)(2,1)} fusion(bf16[45,32,1440]{2,1,0:T(8,128)(2,1)} %get-tuple-element.15, bf16[1,45,32,1440]{3,2,1,0:T(8,128)(2,1)} %param.8), kind=kLoop, calls=%fused_computation.1 | loop fusion | flops 8294400 | bytes 12441600 | tf_op jit(solution)/shard_map/broadcast_in_dim | solution.py:530
  237.9 9.9 %all-to-all-done.5.in_ref = bf16[16,12,24,128]{3,2,1,0:T(8,128)(2,1)S(1)} async-done(((bf16[16,12,24,128]{3,2,1,0:T(8,128)(2,1)}), bf16[16,12,24,128]{3,2,1,0:T(8,128)(2,1)S(1)}, u32[]{:S(2)}, u32[]{:S(2)}) %all-to-all-start.5) | async-done | bytes 1179680 | tf_op jit(solution)/shard_map/all_to_all | solution.py:497
  247.8 0.0 all-gather.7.cloned.1.call-done
  247.8 0.0 copy-start
  247.8 3.7 %copy-done = bf16[24,768,256]{2,1,0:T(8,128)(2,1)S(1)} copy-done((bf16[24,768,256]{2,1,0:T(8,128)(2,1)S(1)}, bf16[24,768,256]{2,1,0:T(8,128)(2,1)}, u32[]{:S(2)}) %copy-start) | copy-done | bytes 9437208
  251.5 3.5 %filter_grad.1 = f32[24,32,256]{2,1,0:T(8,128)} custom-call(bf16[16,12,24,128]{3,2,1,0:T(8,128)(2,1)S(1)} %all-to-all-done.5.in_ref, bf16[8,3,768,256]{3,2,1,0:T(8,128)(2,1)S(1)} %bitcast.9), custom_call_target="tpu_custom_call" | custom-call | flops 6000000000 | bytes 1048576 | tf_op jit(solution)/shard_map/filter_grad/pallas_call | solution.py:480
  (1 shorter events, 0.0 us)
Async XLA Ops:
  7.2 86.7 %all-gather.5.cloned.1.call-start = ((), (), s32[]{:S(2)}) async-start(), calls=%async_computation.6 | async-start | bytes 3538944 | tf_op jit(solution)/shard_map/all_gather | solution.py:517
  17.6 39.4 %copy-start.4 = (s32[192]{0:T(256)S(1)}, s32[192]{0:T(256)}, u32[]{:S(2)}) copy-start(s32[192]{0:T(256)} %pair_ref.9) | copy-start | bytes 2308
  57.0 3.1 %copy-start.1 = (bf16[12,385,720]{2,1,0:T(8,128)(2,1)S(1)}, bf16[12,385,720]{2,1,0:T(8,128)(2,1)}, u32[]{:S(2)}) copy-start(bf16[12,385,720]{2,1,0:T(8,128)(2,1)} %basis_ref.5) | copy-start | bytes 19958404
  65.7 28.1 %all-to-all-start.1 = ((bf16[128,40,128]{2,1,0:T(8,128)(2,1)}), bf16[128,40,128]{2,1,0:T(8,128)(2,1)S(1)}, u32[]{:S(2)}, u32[]{:S(2)}) async-start(bf16[128,40,128]{2,1,0:T(8,128)(2,1)} %analysis.2), calls=%async_computation.1 | async-start | bytes 2621440 | tf_op jit(solution)/shard_map/all_to_all | solution.py:497
  71.9 175.9 %all-gather.7.cloned.1.call-start = ((), (), s32[]{:S(2)}) async-start(), calls=%async_computation.7 | async-start | bytes 10616832 | tf_op jit(solution)/shard_map/all_gather | solution.py:522
  93.8 1.9 copy-start.3
  126.6 3.1 %copy-start.2 = (bf16[12,385,720]{2,1,0:T(8,128)(2,1)S(1)}, bf16[12,385,720]{2,1,0:T(8,128)(2,1)}, u32[]{:S(2)}) copy-start(bf16[12,385,720]{2,1,0:T(8,128)(2,1)} %basis_ref.5) | copy-start | bytes 19958404
  129.7 39.6 %copy-start.5 = (bf16[768,1440]{1,0:T(8,128)(2,1)S(1)}, bf16[768,1440]{1,0:T(8,128)(2,1)}, u32[]{:S(2)}) copy-start(bf16[768,1440]{1,0:T(8,128)(2,1)} %constant.20.table_ref) | copy-start | bytes 6635524
  135.1 86.6 %slice-start = ((s8[7225344]{0:T(1024)(128)(4,1)}), s8[4194304]{0:T(1024)(128)(4,1)S(1)}, s32[]{:S(2)}) async-start(s8[7225344]{0:T(1024)(128)(4,1)} %bitcast.10), calls=%async_computation.8 | async-start | bytes 8388608
  169.3 52.4 %slice-start.1 = ((s8[7225344]{0:T(1024)(128)(4,1)}), s8[3031040]{0:T(1024)(128)(4,1)S(1)}, s32[]{:S(2)}) async-start(s8[7225344]{0:T(1024)(128)(4,1)} %bitcast.10), calls=%async_computation.9 | async-start | bytes 6062080
  226.6 21.2 %all-to-all-start.5 = ((bf16[16,12,24,128]{3,2,1,0:T(8,128)(2,1)}), bf16[16,12,24,128]{3,2,1,0:T(8,128)(2,1)S(1)}, u32[]{:S(2)}, u32[]{:S(2)}) async-start(bf16[16,12,24,128]{3,2,1,0:T(8,128)(2,1)} %analysis.3), calls=%async_computation.5 | async-start | bytes 2359296 | tf_op jit(solution)/shard_map/all_to_all | solution.py:497
  247.8 3.7 %copy-start = (bf16[24,768,256]{2,1,0:T(8,128)(2,1)S(1)}, bf16[24,768,256]{2,1,0:T(8,128)(2,1)}, u32[]{:S(2)}) copy-start(bf16[24,768,256]{2,1,0:T(8,128)(2,1)} %all-gather.7.cloned.1.call-done) | copy-start | bytes 28311556
Sparse Core Ops, SparseCore 0:
  17.8 30.1 all-gather.4
  126.8 49.8 all-gather.6

commit v4 on v3

--- a/solution.py
+++ b/solution.py
@@ -14,7 +14,7 @@
 GROUP = 32
 T_STEP = 16
 T_PART = 8
-S_STEP = 4
+S_STEP = 6
 
 
 def params(mib):
@@ -306,7 +306,7 @@
         out_specs=out_spec,
         out_shape=jax.ShapeDtypeStruct(shape, BF16),
         scratch_shapes=scratch,
-        compiler_params=params(18),
+        compiler_params=params(24),
         cost_estimate=cost(6),
         name="analysis",
     )(*places, arrived, basis)
@@ -367,7 +367,7 @@
             pltpu.VMEM((S_STEP, degrees + 8, 128), F32),
             pltpu.VMEM((S_STEP, lat_total, 128), F32),
         ],
-        compiler_params=params(18),
+        compiler_params=params(24),
         cost_estimate=cost(7),
         name="synthesis",
     )(*places, filtered, basis)
@@ -493,6 +493,10 @@
     )(received, by_degree)
 
 
+def stay(array):
+    return pltpu.with_memory_space_constraint(array, pltpu.HBM)
+
+
 def exchange(array, axis):
     return lax.all_to_all(array, axis, split_axis=0, concat_axis=0, tiled=True)
 
@@ -516,16 +520,16 @@
     )
     weights = lax.all_gather(weights, "chan")
     weights = weights.reshape(chans, degrees // owners // chans, chans, chan_rows, -1)
-    coefficients = analysis(exchange(spectrum, "lat"), legendre_basis, places, True)
+    coefficients = analysis(exchange(spectrum, "lat"), stay(legendre_basis), places, True)
     filtered, by_degree = spectral_filter(exchange(coefficients, everyone), weights, me, slots)
     filtered, by_degree = lax.optimization_barrier((exchange(filtered, everyone), by_degree))
     by_degree = lax.all_gather(by_degree, "chan")
-    lines = synthesize(filtered, legendre_basis, places, owners, lat_rows)
+    lines = synthesize(filtered, stay(legendre_basis), places, owners, lat_rows)
     gate, grads = middle_transform(
         exchange(lines, "lat"), cotangent, pair_list, inverse_table, owners, slots
     )
     grads = analysis(exchange(grads, "lat"), legendre_basis, places, False)
-    weight_grad = filter_grad(exchange(grads, "lat"), by_degree)
+    weight_grad = filter_grad(exchange(grads, "lat"), stay(by_degree))
     block_out = (grid.astype(F32) + gate.astype(F32)).astype(BF16)
     return (block_out[None], weight_grad)
 

time: 262 us -> 258 us (0.985)
  local copies, waits for them, and re-layouts: 11.7 us -> 1.91 us
  Pallas kernels: 53.2 us -> 58.4 us
    unnamed x16 -> x10, local copies, waits for them, and re-layouts: 11.7 us -> 1.91 us
    pallas_call x1, Pallas kernels: 3.46 us -> 6.18 us  [filter_grad(): pl.pallas_call(grad_body, grid=(steps,), in_specs=[pl.BlockSpec(received....]
  transfers between devices with their start and end apart: 4 -> 4, of which waited for: 2 -> 2; matrix products, arithmetic and copies ran while one was open for 3% -> 3% of each run, Pallas kernels for 13% -> 14%
where the time goes in v4:
time: 258 us; the launch traced here: 257 us
  blocking collectives  134 us (52%)
  Pallas kernels  58.4 us (23%)
  waiting for transfers between devices  31.9 us (12%)
  between operations  14.1 us (5%)
  starting transfers between devices  9.89 us (4%)
  other arithmetic  7.56 us (3%)
    all_to_all x4, blocking collectives, exchange(): return lax.all_to_all(array, axis, split_axis=0, concat_axis=0, tiled=True)  134 us
    all_to_all x2, waiting for transfers between devices, exchange(): return lax.all_to_all(array, axis, split_axis=0, concat_axis=0, tiled=True)  31.9 us
    pallas_call x1, Pallas kernels, middle_transform(): pl.pallas_call(functools.partial(middle_body, pairs, slots), grid=(pl.cdi...  18.7 us
    pallas_call x2, Pallas kernels, analysis(): pl.pallas_call(functools.partial(analysis_body, spread), grid=(slots // S...  11.7 us
    pallas_call x1, Pallas kernels, forward_transform(): pl.pallas_call(functools.partial(forward_body, pairs, slots, lat_rows), g...  10.4 us
    all_to_all x2, starting transfers between devices, exchange(): return lax.all_to_all(array, axis, split_axis=0, concat_axis=0, tiled=True)  9.81 us
    broadcast_in_dim x1, other arithmetic, on_device(): return (block_out[None], weight_grad)  7.56 us
    pallas_call x1, Pallas kernels, synthesize(): pl.pallas_call(synthesis_body, grid=(slots // S_STEP,), in_specs=[pl.Bloc...  6.75 us
  transfers between devices with their start and end apart: 4, of which 2 were waited for; matrix products, arithmetic and copies ran while one was open for 3% of the time, Pallas kernels for 14%

profile of v4, /device:TPU:0, one launch (start us, length us, event | category | flops | bytes accessed | tf_op | source)
XLA Modules:
  0.0 257.3 jit_solution(10368046142645428470)
XLA Ops:
  7.2 0.0 all-gather.5.cloned.1.call-start
  7.2 10.4 %forward_transform.1 = (bf16[16,12,45,128]{3,2,1,0:T(8,128)(2,1)}, bf16[24,32,256]{2,1,0:T(8,128)(2,1)}) custom-call(s32[1]{0:T(128)} %bitcast.1.owner_ref, s32[192]{0:T(256)} %pair_ref.9, f32[45]{0:T(128)} %weight_ref.1, bf16[45,32,1440]{2,1,0:T(8,128)(2,1)} %bitcast.12, bf16[768,1440]{1,0:T(8,128)(2,1)} %constant.19.refs_1_, bf16[384,32,256]{2,1,0:T(8,128)(2,1)} %refs_2_.1), custom_call_target="tpu_custom_call" | custom-call | flops 12000000000 | bytes 1048576 | tf_op jit(solution)/shard_map/forward_transform/pallas_call | solution.py:140
  17.6 0.0 all-gather.5.cloned.1.call-update
  17.6 0.0 copy-start.1
  17.7 39.3 %all_to_all.30.in_ref = bf16[16,12,45,128]{3,2,1,0:T(8,128)(2,1)S(1)} all-to-all(bf16[16,12,45,128]{3,2,1,0:T(8,128)(2,1)} %get-tuple-element.10), channel_id=1, replica_groups=mesh['lat'=16,'chan'=8] {'lat'}, dimensions={0} | all-to-all | bytes 4423680 | tf_op jit(solution)/shard_map/all_to_all | solution.py:501
  57.0 0.0 copy-done.1
  57.0 6.9 %analysis.2 = bf16[128,40,128]{2,1,0:T(8,128)(2,1)} custom-call(s32[1]{0:T(128)} %bitcast.1.owner_ref, s32[192]{0:T(256)S(1)} %copy-done.1, bf16[16,12,45,128]{3,2,1,0:T(8,128)(2,1)S(1)} %all_to_all.30.in_ref, bf16[12,385,720]{2,1,0:T(8,128)(2,1)} %basis_ref.5), custom_call_target="tpu_custom_call" | custom-call | flops 6000000000 | bytes 1048576 | tf_op jit(solution)/shard_map/analysis/pallas_call | solution.py:297
  63.9 6.1 %all-to-all-start.1 = ((bf16[128,40,128]{2,1,0:T(8,128)(2,1)}), bf16[128,40,128]{2,1,0:T(8,128)(2,1)S(1)}, u32[]{:S(2)}, u32[]{:S(2)}) async-start(bf16[128,40,128]{2,1,0:T(8,128)(2,1)} %analysis.2), calls=%async_computation.1 | async-start | bytes 2621440 | tf_op jit(solution)/shard_map/all_to_all | solution.py:501
  70.0 0.0 all-gather.7.cloned.1.call-start
  70.1 21.9 %all-to-all-done.1.in_ref = bf16[128,40,128]{2,1,0:T(8,128)(2,1)S(1)} async-done(((bf16[128,40,128]{2,1,0:T(8,128)(2,1)}), bf16[128,40,128]{2,1,0:T(8,128)(2,1)S(1)}, u32[]{:S(2)}, u32[]{:S(2)}) %all-to-all-start.1) | async-done | bytes 1310752 | tf_op jit(solution)/shard_map/all_to_all | solution.py:501
  92.0 0.0 all-gather.5.cloned.1.call-done
  92.0 0.0 copy-start
  92.0 1.9 copy-done
  93.9 4.7 %spectral_filter.1 = (bf16[128,40,128]{2,1,0:T(8,128)(2,1)S(1)}, bf16[3,768,256]{2,1,0:T(8,128)(2,1)}) custom-call(s32[1]{0:T(128)} %bitcast.2.me_ref, bf16[128,40,128]{2,1,0:T(8,128)(2,1)S(1)} %all-to-all-done.1.in_ref, bf16[8,3,8,32,256]{4,3,2,1,0:T(8,128)(2,1)S(1)} %bitcast.11), custom_call_target="tpu_custom_call" | custom-call | flops 6000000000 | bytes 1048576 | tf_op jit(solution)/shard_map/spectral_filter/pallas_call | solution.py:434
  98.6 26.2 %all_to_all.31.in_ref = bf16[128,40,128]{2,1,0:T(8,128)(2,1)S(1)} all-to-all(bf16[128,40,128]{2,1,0:T(8,128)(2,1)S(1)} %get-tuple-element.12), channel_id=1, replica_groups=mesh['lat'=16,'chan'=8] {'lat','chan'}, dimensions={0} | all-to-all | bytes 2621440 | tf_op jit(solution)/shard_map/all_to_all | solution.py:501
  124.8 0.0 all-gather.7.cloned.1.call-update
  124.8 0.0 copy-start.2
  124.8 6.8 %synthesis.1 = bf16[16,12,45,128]{3,2,1,0:T(8,128)(2,1)S(1)} custom-call(s32[1]{0:T(128)} %bitcast.1.owner_ref, s32[192]{0:T(256)S(1)} %copy-done.1, bf16[128,40,128]{2,1,0:T(8,128)(2,1)S(1)} %all_to_all.31.in_ref, bf16[12,385,720]{2,1,0:T(8,128)(2,1)} %basis_ref.5), custom_call_target="tpu_custom_call" | custom-call | flops 7000000000 | bytes 1048576 | tf_op jit(solution)/shard_map/synthesis/pallas_call | solution.py:354
  131.6 0.0 slice-start
  131.6 34.3 %all_to_all.32.in_ref = bf16[16,12,45,128]{3,2,1,0:T(8,128)(2,1)S(1)} all-to-all(bf16[16,12,45,128]{3,2,1,0:T(8,128)(2,1)S(1)} %synthesis.1), channel_id=1, replica_groups=mesh['lat'=16,'chan'=8] {'lat'}, dimensions={0} | all-to-all | bytes 4423680 | tf_op jit(solution)/shard_map/all_to_all | solution.py:501
  165.9 0.0 copy-done.2
  165.9 0.0 slice-start.1
  165.9 18.7 %middle_transform.1 = (bf16[45,32,1440]{2,1,0:T(8,128)(2,1)}, bf16[16,12,45,128]{3,2,1,0:T(8,128)(2,1)S(1)}) custom-call(s32[192]{0:T(256)S(1)} %copy-done.1, bf16[16,12,45,128]{3,2,1,0:T(8,128)(2,1)S(1)} %all_to_all.32.in_ref, bf16[45,32,1440]{2,1,0:T(8,128)(2,1)} %bitcast.14, bf16[768,1440]{1,0:T(8,128)(2,1)S(1)} %copy-done.2), custom_call_target="tpu_custom_call" | custom-call | flops 24999999488 | bytes 1048576 | tf_op jit(solution)/shard_map/middle_transform/pallas_call | solution.py:204
  184.6 33.7 %all_to_all.33.in_ref = bf16[16,12,45,128]{3,2,1,0:T(8,128)(2,1)S(1)} all-to-all(bf16[16,12,45,128]{3,2,1,0:T(8,128)(2,1)S(1)} %get-tuple-element.16), channel_id=1, replica_groups=mesh['lat'=16,'chan'=8] {'lat'}, dimensions={0} | all-to-all | bytes 4423680 | tf_op jit(solution)/shard_map/all_to_all | solution.py:501
  218.3 0.0 slice-done
  218.3 0.0 slice-done.1
  218.3 4.8 %analysis.3 = bf16[16,12,24,128]{3,2,1,0:T(8,128)(2,1)} custom-call(s32[1]{0:T(128)} %bitcast.1.owner_ref, s32[192]{0:T(256)S(1)} %copy-done.1, bf16[16,12,45,128]{3,2,1,0:T(8,128)(2,1)S(1)} %all_to_all.33.in_ref, bf16[12,385,720]{2,1,0:T(8,128)(2,1)S(1)} %bitcast.10), custom_call_target="tpu_custom_call" | custom-call | flops 6000000000 | bytes 1048576 | tf_op jit(solution)/shard_map/analysis/pallas_call | solution.py:297
  223.1 3.7 %all-to-all-start.5 = ((bf16[16,12,24,128]{3,2,1,0:T(8,128)(2,1)}), bf16[16,12,24,128]{3,2,1,0:T(8,128)(2,1)S(1)}, u32[]{:S(2)}, u32[]{:S(2)}) async-start(bf16[16,12,24,128]{3,2,1,0:T(8,128)(2,1)} %analysis.3), calls=%async_computation.5 | async-start | bytes 2359296 | tf_op jit(solution)/shard_map/all_to_all | solution.py:501
  226.8 7.6 %fusion = bf16[1,45,32,1440]{3,2,1,0:T(8,128)(2,1)} fusion(bf16[45,32,1440]{2,1,0:T(8,128)(2,1)} %get-tuple-element.15, bf16[1,45,32,1440]{3,2,1,0:T(8,128)(2,1)} %param.8), kind=kLoop, calls=%fused_computation.1 | loop fusion | flops 8294400 | bytes 12441600 | tf_op jit(solution)/shard_map/broadcast_in_dim | solution.py:534
  234.4 9.9 %all-to-all-done.5.in_ref = bf16[16,12,24,128]{3,2,1,0:T(8,128)(2,1)S(1)} async-done(((bf16[16,12,24,128]{3,2,1,0:T(8,128)(2,1)}), bf16[16,12,24,128]{3,2,1,0:T(8,128)(2,1)S(1)}, u32[]{:S(2)}, u32[]{:S(2)}) %all-to-all-start.5) | async-done | bytes 1179680 | tf_op jit(solution)/shard_map/all_to_all | solution.py:501
  244.3 0.0 all-gather.7.cloned.1.call-done
  244.3 6.2 %filter_grad.1 = f32[24,32,256]{2,1,0:T(8,128)} custom-call(bf16[16,12,24,128]{3,2,1,0:T(8,128)(2,1)S(1)} %all-to-all-done.5.in_ref, bf16[8,3,768,256]{3,2,1,0:T(8,128)(2,1)} %bitcast.13), custom_call_target="tpu_custom_call" | custom-call | flops 6000000000 | bytes 1048576 | tf_op jit(solution)/shard_map/filter_grad/pallas_call | solution.py:480
  (1 shorter events, 0.0 us)
Async XLA Ops:
  7.2 84.8 %all-gather.5.cloned.1.call-start = ((), (), s32[]{:S(2)}) async-start(), calls=%async_computation.6 | async-start | bytes 3538944 | tf_op jit(solution)/shard_map/all_gather | solution.py:521
  17.6 39.4 %copy-start.1 = (s32[192]{0:T(256)S(1)}, s32[192]{0:T(256)}, u32[]{:S(2)}) copy-start(s32[192]{0:T(256)} %pair_ref.9) | copy-start | bytes 2308
  63.9 28.1 %all-to-all-start.1 = ((bf16[128,40,128]{2,1,0:T(8,128)(2,1)}), bf16[128,40,128]{2,1,0:T(8,128)(2,1)S(1)}, u32[]{:S(2)}, u32[]{:S(2)}) async-start(bf16[128,40,128]{2,1,0:T(8,128)(2,1)} %analysis.2), calls=%async_computation.1 | async-start | bytes 2621440 | tf_op jit(solution)/shard_map/all_to_all | solution.py:501
  70.0 174.3 %all-gather.7.cloned.1.call-start = ((), (), s32[]{:S(2)}) async-start(), calls=%async_computation.7 | async-start | bytes 10616832 | tf_op jit(solution)/shard_map/all_gather | solution.py:526
  92.0 1.9 copy-start
  124.8 41.1 %copy-start.2 = (bf16[768,1440]{1,0:T(8,128)(2,1)S(1)}, bf16[768,1440]{1,0:T(8,128)(2,1)}, u32[]{:S(2)}) copy-start(bf16[768,1440]{1,0:T(8,128)(2,1)} %constant.20.table_ref) | copy-start | bytes 6635524
  131.6 86.8 %slice-start = ((s8[7225344]{0:T(1024)(128)(4,1)}), s8[4194304]{0:T(1024)(128)(4,1)S(1)}, s32[]{:S(2)}) async-start(s8[7225344]{0:T(1024)(128)(4,1)} %bitcast.9), calls=%async_computation.8 | async-start | bytes 8388608
  165.9 52.4 %slice-start.1 = ((s8[7225344]{0:T(1024)(128)(4,1)}), s8[3031040]{0:T(1024)(128)(4,1)S(1)}, s32[]{:S(2)}) async-start(s8[7225344]{0:T(1024)(128)(4,1)} %bitcast.9), calls=%async_computation.9 | async-start | bytes 6062080
  223.1 21.2 %all-to-all-start.5 = ((bf16[16,12,24,128]{3,2,1,0:T(8,128)(2,1)}), bf16[16,12,24,128]{3,2,1,0:T(8,128)(2,1)S(1)}, u32[]{:S(2)}, u32[]{:S(2)}) async-start(bf16[16,12,24,128]{3,2,1,0:T(8,128)(2,1)} %analysis.3), calls=%async_computation.5 | async-start | bytes 2359296 | tf_op jit(solution)/shard_map/all_to_all | solution.py:501
Sparse Core Ops, SparseCore 0:
  17.8 30.1 all-gather.4
  124.9 49.8 all-gather.6

commit v5 on v4

--- a/solution.py
+++ b/solution.py
@@ -129,7 +129,7 @@
 def turn_scratch(pairs):
     return [
         pltpu.VMEM((T_STEP // T_PART, 4 * pairs, T_PART * GROUP), F32),
-        pltpu.VMEM((T_STEP * (pairs + PAD), 128), F32),
+        pltpu.VMEM((round_up((T_STEP + 1) * (pairs + PAD), 8), 128), F32),
     ]
 
 
@@ -274,7 +274,8 @@
 
         @pl.when(step == pl.num_programs(0) - 1)
         def _():
-            out_ref[...] = sent_ref[...].astype(BF16).reshape(out_ref.shape)
+            sent = sent_ref[: out_ref.shape[0] * out_ref.shape[1], :]
+            out_ref[...] = sent.astype(BF16).reshape(out_ref.shape)
 
 
 def analysis(arrived, basis, places, spread):
@@ -289,7 +290,7 @@
         block_rows = round_up(3 * slots, 8)
         shape = (owners * 8, block_rows, 128)
         out_spec = pl.BlockSpec(shape, lambda k: (0, 0, 0))
-        scratch.append(pltpu.VMEM((owners * 8 * block_rows, 128), F32))
+        scratch.append(pltpu.VMEM(((owners * 8 + 1) * block_rows, 128), F32))
     else:
         part = degrees // owners
         shape = (owners, slots, part, 128)
@@ -323,7 +324,7 @@
 
     @pl.when(step == 0)
     def _():
-        held_ref[...] = in_ref[...].astype(F32).reshape(held_ref.shape)
+        held_ref[: in_ref.shape[0] * block_rows, :] = in_ref[...].astype(F32).reshape(-1, 128)
         rows_ref[...] = jnp.zeros_like(rows_ref)
 
     for k in range(steps):
@@ -363,7 +364,7 @@
         out_specs=pl.BlockSpec((owners, S_STEP, lat_rows, 128), lambda k: (0, k, 0, 0)),
         out_shape=jax.ShapeDtypeStruct((owners, slots, lat_rows, 128), BF16),
         scratch_shapes=[
-            pltpu.VMEM((devices * block_rows, 128), F32),
+            pltpu.VMEM(((devices + 1) * block_rows, 128), F32),
             pltpu.VMEM((S_STEP, degrees + 8, 128), F32),
             pltpu.VMEM((S_STEP, lat_total, 128), F32),
         ],
@@ -442,8 +443,8 @@
             ],
             out_specs=[whole(received.shape), whole(degree_shape)],
             scratch_shapes=[
-                pltpu.VMEM((4, 2, owners * HELD, 128), F32),
-                pltpu.VMEM((4, 2, owners * HELD, 128), F32),
+                pltpu.VMEM((4, 2, owners * HELD + 8, 128), F32),
+                pltpu.VMEM((4, 2, owners * HELD + 8, 128), F32),
                 pltpu.VMEM((4 * owners * slots, 256), F32),
             ],
         ),
@@ -463,7 +464,7 @@
 
     @pl.when(step == 0)
     def _():
-        rows_ref[...] = in_ref[...].astype(F32).reshape(rows_ref.shape)
+        rows_ref[: owners * slots * part, :] = in_ref[...].astype(F32).reshape(-1, 128)
 
     group = lax.broadcasted_iota(jnp.int32, (owners * slots, 128), 1) // GROUP
     for j in range(8):
@@ -486,7 +487,7 @@
         ],
         out_specs=pl.BlockSpec((chans, GROUP, 256), lambda s: (s, 0, 0)),
         out_shape=jax.ShapeDtypeStruct((part, GROUP, 256), F32),
-        scratch_shapes=[pltpu.VMEM((owners * slots * part, 128), F32)],
+        scratch_shapes=[pltpu.VMEM(((owners * slots + 1) * part, 128), F32)],
         compiler_params=params(40),
         cost_estimate=cost(6),
         name="filter_grad",

time: 258 us -> 258 us (level)
  no operation moved by 1% of the time
where the time goes in v5:
time: 258 us; the launch traced here: 257 us
  blocking collectives  134 us (52%)
  Pallas kernels  58.4 us (23%)
  waiting for transfers between devices  31.9 us (12%)
  between operations  14.1 us (5%)
  starting transfers between devices  9.88 us (4%)
  other arithmetic  7.56 us (3%)
    all_to_all x4, blocking collectives, exchange(): return lax.all_to_all(array, axis, split_axis=0, concat_axis=0, tiled=True)  134 us
    all_to_all x2, waiting for transfers between devices, exchange(): return lax.all_to_all(array, axis, split_axis=0, concat_axis=0, tiled=True)  31.9 us
    pallas_call x1, Pallas kernels, middle_transform(): pl.pallas_call(functools.partial(middle_body, pairs, slots), grid=(pl.cdi...  18.7 us
    pallas_call x2, Pallas kernels, analysis(): pl.pallas_call(functools.partial(analysis_body, spread), grid=(slots // S...  11.7 us
    pallas_call x1, Pallas kernels, forward_transform(): pl.pallas_call(functools.partial(forward_body, pairs, slots, lat_rows), g...  10.4 us
    all_to_all x2, starting transfers between devices, exchange(): return lax.all_to_all(array, axis, split_axis=0, concat_axis=0, tiled=True)  9.8 us
    broadcast_in_dim x1, other arithmetic, on_device(): return (block_out[None], weight_grad)  7.56 us
    pallas_call x1, Pallas kernels, synthesize(): pl.pallas_call(synthesis_body, grid=(slots // S_STEP,), in_specs=[pl.Bloc...  6.75 us
  transfers between devices with their start and end apart: 4, of which 2 were waited for; matrix products, arithmetic and copies ran while one was open for 3% of the time, Pallas kernels for 14%

profile of v5, /device:TPU:0, one launch (start us, length us, event | category | flops | bytes accessed | tf_op | source)
XLA Modules:
  0.0 257.3 jit_solution(4614391049235757821)
XLA Ops:
  7.2 0.0 all-gather.5.cloned.1.call-start
  7.2 10.4 %forward_transform.1 = (bf16[16,12,45,128]{3,2,1,0:T(8,128)(2,1)}, bf16[24,32,256]{2,1,0:T(8,128)(2,1)}) custom-call(s32[1]{0:T(128)} %bitcast.1.owner_ref, s32[192]{0:T(256)} %pair_ref.9, f32[45]{0:T(128)} %weight_ref.1, bf16[45,32,1440]{2,1,0:T(8,128)(2,1)} %bitcast.12, bf16[768,1440]{1,0:T(8,128)(2,1)} %constant.19.refs_1_, bf16[384,32,256]{2,1,0:T(8,128)(2,1)} %refs_2_.1), custom_call_target="tpu_custom_call" | custom-call | flops 12000000000 | bytes 1048576 | tf_op jit(solution)/shard_map/forward_transform/pallas_call | solution.py:140
  17.6 0.0 all-gather.5.cloned.1.call-update
  17.7 0.0 copy-start.1
  17.7 39.3 %all_to_all.30.in_ref = bf16[16,12,45,128]{3,2,1,0:T(8,128)(2,1)S(1)} all-to-all(bf16[16,12,45,128]{3,2,1,0:T(8,128)(2,1)} %get-tuple-element.10), channel_id=1, replica_groups=mesh['lat'=16,'chan'=8] {'lat'}, dimensions={0} | all-to-all | bytes 4423680 | tf_op jit(solution)/shard_map/all_to_all | solution.py:502
  57.0 0.0 copy-done.1
  57.0 6.9 %analysis.2 = bf16[128,40,128]{2,1,0:T(8,128)(2,1)} custom-call(s32[1]{0:T(128)} %bitcast.1.owner_ref, s32[192]{0:T(256)S(1)} %copy-done.1, bf16[16,12,45,128]{3,2,1,0:T(8,128)(2,1)S(1)} %all_to_all.30.in_ref, bf16[12,385,720]{2,1,0:T(8,128)(2,1)} %basis_ref.5), custom_call_target="tpu_custom_call" | custom-call | flops 6000000000 | bytes 1048576 | tf_op jit(solution)/shard_map/analysis/pallas_call | solution.py:298
  63.9 6.1 %all-to-all-start.1 = ((bf16[128,40,128]{2,1,0:T(8,128)(2,1)}), bf16[128,40,128]{2,1,0:T(8,128)(2,1)S(1)}, u32[]{:S(2)}, u32[]{:S(2)}) async-start(bf16[128,40,128]{2,1,0:T(8,128)(2,1)} %analysis.2), calls=%async_computation.1 | async-start | bytes 2621440 | tf_op jit(solution)/shard_map/all_to_all | solution.py:502
  70.0 0.0 all-gather.7.cloned.1.call-start
  70.1 21.9 %all-to-all-done.1.in_ref = bf16[128,40,128]{2,1,0:T(8,128)(2,1)S(1)} async-done(((bf16[128,40,128]{2,1,0:T(8,128)(2,1)}), bf16[128,40,128]{2,1,0:T(8,128)(2,1)S(1)}, u32[]{:S(2)}, u32[]{:S(2)}) %all-to-all-start.1) | async-done | bytes 1310752 | tf_op jit(solution)/shard_map/all_to_all | solution.py:502
  92.0 0.0 all-gather.5.cloned.1.call-done
  92.0 0.0 copy-start
  92.0 1.9 copy-done
  93.9 4.7 %spectral_filter.1 = (bf16[128,40,128]{2,1,0:T(8,128)(2,1)S(1)}, bf16[3,768,256]{2,1,0:T(8,128)(2,1)}) custom-call(s32[1]{0:T(128)} %bitcast.2.me_ref, bf16[128,40,128]{2,1,0:T(8,128)(2,1)S(1)} %all-to-all-done.1.in_ref, bf16[8,3,8,32,256]{4,3,2,1,0:T(8,128)(2,1)S(1)} %bitcast.11), custom_call_target="tpu_custom_call" | custom-call | flops 6000000000 | bytes 1048576 | tf_op jit(solution)/shard_map/spectral_filter/pallas_call | solution.py:435
  98.5 26.2 %all_to_all.31.in_ref = bf16[128,40,128]{2,1,0:T(8,128)(2,1)S(1)} all-to-all(bf16[128,40,128]{2,1,0:T(8,128)(2,1)S(1)} %get-tuple-element.12), channel_id=1, replica_groups=mesh['lat'=16,'chan'=8] {'lat','chan'}, dimensions={0} | all-to-all | bytes 2621440 | tf_op jit(solution)/shard_map/all_to_all | solution.py:502
  124.7 0.0 all-gather.7.cloned.1.call-update
  124.8 0.0 copy-start.2
  124.8 6.8 %synthesis.1 = bf16[16,12,45,128]{3,2,1,0:T(8,128)(2,1)S(1)} custom-call(s32[1]{0:T(128)} %bitcast.1.owner_ref, s32[192]{0:T(256)S(1)} %copy-done.1, bf16[128,40,128]{2,1,0:T(8,128)(2,1)S(1)} %all_to_all.31.in_ref, bf16[12,385,720]{2,1,0:T(8,128)(2,1)} %basis_ref.5), custom_call_target="tpu_custom_call" | custom-call | flops 7000000000 | bytes 1048576 | tf_op jit(solution)/shard_map/synthesis/pallas_call | solution.py:355
  131.5 0.0 slice-start
  131.6 34.3 %all_to_all.32.in_ref = bf16[16,12,45,128]{3,2,1,0:T(8,128)(2,1)S(1)} all-to-all(bf16[16,12,45,128]{3,2,1,0:T(8,128)(2,1)S(1)} %synthesis.1), channel_id=1, replica_groups=mesh['lat'=16,'chan'=8] {'lat'}, dimensions={0} | all-to-all | bytes 4423680 | tf_op jit(solution)/shard_map/all_to_all | solution.py:502
  165.9 0.0 copy-done.2
  165.9 0.0 slice-start.1
  165.9 18.7 %middle_transform.1 = (bf16[45,32,1440]{2,1,0:T(8,128)(2,1)}, bf16[16,12,45,128]{3,2,1,0:T(8,128)(2,1)S(1)}) custom-call(s32[192]{0:T(256)S(1)} %copy-done.1, bf16[16,12,45,128]{3,2,1,0:T(8,128)(2,1)S(1)} %all_to_all.32.in_ref, bf16[45,32,1440]{2,1,0:T(8,128)(2,1)} %bitcast.14, bf16[768,1440]{1,0:T(8,128)(2,1)S(1)} %copy-done.2), custom_call_target="tpu_custom_call" | custom-call | flops 24999999488 | bytes 1048576 | tf_op jit(solution)/shard_map/middle_transform/pallas_call | solution.py:204
  184.6 33.7 %all_to_all.33.in_ref = bf16[16,12,45,128]{3,2,1,0:T(8,128)(2,1)S(1)} all-to-all(bf16[16,12,45,128]{3,2,1,0:T(8,128)(2,1)S(1)} %get-tuple-element.16), channel_id=1, replica_groups=mesh['lat'=16,'chan'=8] {'lat'}, dimensions={0} | all-to-all | bytes 4423680 | tf_op jit(solution)/shard_map/all_to_all | solution.py:502
  218.3 0.0 slice-done
  218.3 0.0 slice-done.1
  218.3 4.8 %analysis.3 = bf16[16,12,24,128]{3,2,1,0:T(8,128)(2,1)} custom-call(s32[1]{0:T(128)} %bitcast.1.owner_ref, s32[192]{0:T(256)S(1)} %copy-done.1, bf16[16,12,45,128]{3,2,1,0:T(8,128)(2,1)S(1)} %all_to_all.33.in_ref, bf16[12,385,720]{2,1,0:T(8,128)(2,1)S(1)} %bitcast.10), custom_call_target="tpu_custom_call" | custom-call | flops 6000000000 | bytes 1048576 | tf_op jit(solution)/shard_map/analysis/pallas_call | solution.py:298
  223.1 3.7 %all-to-all-start.5 = ((bf16[16,12,24,128]{3,2,1,0:T(8,128)(2,1)}), bf16[16,12,24,128]{3,2,1,0:T(8,128)(2,1)S(1)}, u32[]{:S(2)}, u32[]{:S(2)}) async-start(bf16[16,12,24,128]{3,2,1,0:T(8,128)(2,1)} %analysis.3), calls=%async_computation.5 | async-start | bytes 2359296 | tf_op jit(solution)/shard_map/all_to_all | solution.py:502
  226.8 7.6 %fusion = bf16[1,45,32,1440]{3,2,1,0:T(8,128)(2,1)} fusion(bf16[45,32,1440]{2,1,0:T(8,128)(2,1)} %get-tuple-element.15, bf16[1,45,32,1440]{3,2,1,0:T(8,128)(2,1)} %param.8), kind=kLoop, calls=%fused_computation.1 | loop fusion | flops 8294400 | bytes 12441600 | tf_op jit(solution)/shard_map/broadcast_in_dim | solution.py:535
  234.4 10.0 %all-to-all-done.5.in_ref = bf16[16,12,24,128]{3,2,1,0:T(8,128)(2,1)S(1)} async-done(((bf16[16,12,24,128]{3,2,1,0:T(8,128)(2,1)}), bf16[16,12,24,128]{3,2,1,0:T(8,128)(2,1)S(1)}, u32[]{:S(2)}, u32[]{:S(2)}) %all-to-all-start.5) | async-done | bytes 1179680 | tf_op jit(solution)/shard_map/all_to_all | solution.py:502
  244.3 0.0 all-gather.7.cloned.1.call-done
  244.3 6.2 %filter_grad.1 = f32[24,32,256]{2,1,0:T(8,128)} custom-call(bf16[16,12,24,128]{3,2,1,0:T(8,128)(2,1)S(1)} %all-to-all-done.5.in_ref, bf16[8,3,768,256]{3,2,1,0:T(8,128)(2,1)} %bitcast.13), custom_call_target="tpu_custom_call" | custom-call | flops 6000000000 | bytes 1048576 | tf_op jit(solution)/shard_map/filter_grad/pallas_call | solution.py:481
  (1 shorter events, 0.0 us)
Async XLA Ops:
  7.2 84.8 %all-gather.5.cloned.1.call-start = ((), (), s32[]{:S(2)}) async-start(), calls=%async_computation.6 | async-start | bytes 3538944 | tf_op jit(solution)/shard_map/all_gather | solution.py:522
  17.7 39.4 %copy-start.1 = (s32[192]{0:T(256)S(1)}, s32[192]{0:T(256)}, u32[]{:S(2)}) copy-start(s32[192]{0:T(256)} %pair_ref.9) | copy-start | bytes 2308
  63.9 28.1 %all-to-all-start.1 = ((bf16[128,40,128]{2,1,0:T(8,128)(2,1)}), bf16[128,40,128]{2,1,0:T(8,128)(2,1)S(1)}, u32[]{:S(2)}, u32[]{:S(2)}) async-start(bf16[128,40,128]{2,1,0:T(8,128)(2,1)} %analysis.2), calls=%async_computation.1 | async-start | bytes 2621440 | tf_op jit(solution)/shard_map/all_to_all | solution.py:502
  70.0 174.3 %all-gather.7.cloned.1.call-start = ((), (), s32[]{:S(2)}) async-start(), calls=%async_computation.7 | async-start | bytes 10616832 | tf_op jit(solution)/shard_map/all_gather | solution.py:527
  92.0 1.9 copy-start
  124.8 41.1 %copy-start.2 = (bf16[768,1440]{1,0:T(8,128)(2,1)S(1)}, bf16[768,1440]{1,0:T(8,128)(2,1)}, u32[]{:S(2)}) copy-start(bf16[768,1440]{1,0:T(8,128)(2,1)} %constant.20.table_ref) | copy-start | bytes 6635524
  131.5 86.8 %slice-start = ((s8[7225344]{0:T(1024)(128)(4,1)}), s8[4194304]{0:T(1024)(128)(4,1)S(1)}, s32[]{:S(2)}) async-start(s8[7225344]{0:T(1024)(128)(4,1)} %bitcast.9), calls=%async_computation.8 | async-start | bytes 8388608
  165.9 52.5 %slice-start.1 = ((s8[7225344]{0:T(1024)(128)(4,1)}), s8[3031040]{0:T(1024)(128)(4,1)S(1)}, s32[]{:S(2)}) async-start(s8[7225344]{0:T(1024)(128)(4,1)} %bitcast.9), calls=%async_computation.9 | async-start | bytes 6062080
  223.1 21.2 %all-to-all-start.5 = ((bf16[16,12,24,128]{3,2,1,0:T(8,128)(2,1)}), bf16[16,12,24,128]{3,2,1,0:T(8,128)(2,1)S(1)}, u32[]{:S(2)}, u32[]{:S(2)}) async-start(bf16[16,12,24,128]{3,2,1,0:T(8,128)(2,1)} %analysis.3), calls=%async_computation.5 | async-start | bytes 2359296 | tf_op jit(solution)/shard_map/all_to_all | solution.py:502
Sparse Core Ops, SparseCore 0:
  17.8 30.1 all-gather.4
  124.9 49.8 all-gather.6

commit v6 on v5

--- a/solution.py
+++ b/solution.py
@@ -13,7 +13,7 @@
 BF16 = jnp.bfloat16
 GROUP = 32
 T_STEP = 16
-T_PART = 8
+T_PART = 16
 S_STEP = 6
 
 
@@ -230,7 +230,7 @@
     return [divmod(tile, degrees // chans // owners) for tile in range(degrees // chans)]
 
 
-def analysis_body(spread, owner_ref, pair_ref, in_ref, basis_ref, out_ref, lats_ref, rows_ref, *refs):
+def analysis_body(spread, used_rows, owner_ref, pair_ref, in_ref, basis_ref, out_ref, lats_ref, rows_ref, *refs):
     step = pl.program_id(0)
     owners, steps, lat_rows, _ = in_ref.shape
     degrees = basis_ref.shape[1] - 1
@@ -242,7 +242,9 @@
 
         @pl.when(step == 0)
         def _():
-            sent_ref[...] = jnp.zeros_like(sent_ref)
+            devices, block_rows, _ = out_ref.shape
+            for row in range(used_rows, block_rows):
+                sent_ref[pl.ds(row, devices, stride=block_rows), :] = jnp.zeros((devices, 128), F32)
 
     for k in range(steps):
         for owner in range(owners):
@@ -296,7 +298,7 @@
         shape = (owners, slots, part, 128)
         out_spec = pl.BlockSpec((owners, S_STEP, part, 128), lambda k: (0, k, 0, 0))
     return pl.pallas_call(
-        functools.partial(analysis_body, spread),
+        functools.partial(analysis_body, spread, 3 * slots),
         grid=(slots // S_STEP,),
         in_specs=[
             pl.BlockSpec(memory_space=pltpu.SMEM),
@@ -325,7 +327,7 @@
     @pl.when(step == 0)
     def _():
         held_ref[: in_ref.shape[0] * block_rows, :] = in_ref[...].astype(F32).reshape(-1, 128)
-        rows_ref[...] = jnp.zeros_like(rows_ref)
+        rows_ref[:, degrees:, :] = jnp.zeros((steps, size - degrees, 128), F32)
 
     for k in range(steps):
         slot = step * steps + k

time: 258 us -> 258 us (level)
  no operation moved by 1% of the time
where the time goes in v6:
time: 258 us; the launch traced here: 257 us
  blocking collectives  134 us (52%)
  Pallas kernels  58.3 us (23%)
  waiting for transfers between devices  31.9 us (12%)
  between operations  14.1 us (5%)
  starting transfers between devices  9.89 us (4%)
  other arithmetic  7.56 us (3%)
    all_to_all x4, blocking collectives, exchange(): return lax.all_to_all(array, axis, split_axis=0, concat_axis=0, tiled=True)  134 us
    all_to_all x2, waiting for transfers between devices, exchange(): return lax.all_to_all(array, axis, split_axis=0, concat_axis=0, tiled=True)  31.9 us
    pallas_call x1, Pallas kernels, middle_transform(): pl.pallas_call(functools.partial(middle_body, pairs, slots), grid=(pl.cdi...  18.7 us
    pallas_call x2, Pallas kernels, analysis(): pl.pallas_call(functools.partial(analysis_body, spread, 3 * slots), grid=...  11.6 us
    pallas_call x1, Pallas kernels, forward_transform(): pl.pallas_call(functools.partial(forward_body, pairs, slots, lat_rows), g...  10.4 us
    all_to_all x2, starting transfers between devices, exchange(): return lax.all_to_all(array, axis, split_axis=0, concat_axis=0, tiled=True)  9.81 us
    broadcast_in_dim x1, other arithmetic, on_device(): return (block_out[None], weight_grad)  7.56 us
    pallas_call x1, Pallas kernels, synthesize(): pl.pallas_call(synthesis_body, grid=(slots // S_STEP,), in_specs=[pl.Bloc...  6.68 us
  transfers between devices with their start and end apart: 4, of which 2 were waited for; matrix products, arithmetic and copies ran while one was open for 3% of the time, Pallas kernels for 14%

profile of v6, /device:TPU:0, one launch (start us, length us, event | category | flops | bytes accessed | tf_op | source)
XLA Modules:
  0.0 257.2 jit_solution(9564845955672448715)
XLA Ops:
  7.2 0.0 all-gather.5.cloned.1.call-start
  7.2 10.4 %forward_transform.1 = (bf16[16,12,45,128]{3,2,1,0:T(8,128)(2,1)}, bf16[24,32,256]{2,1,0:T(8,128)(2,1)}) custom-call(s32[1]{0:T(128)} %bitcast.1.owner_ref, s32[192]{0:T(256)} %pair_ref.9, f32[45]{0:T(128)} %weight_ref.1, bf16[45,32,1440]{2,1,0:T(8,128)(2,1)} %bitcast.12, bf16[768,1440]{1,0:T(8,128)(2,1)} %constant.19.refs_1_, bf16[384,32,256]{2,1,0:T(8,128)(2,1)} %refs_2_.1), custom_call_target="tpu_custom_call" | custom-call | flops 12000000000 | bytes 1048576 | tf_op jit(solution)/shard_map/forward_transform/pallas_call | solution.py:140
  17.6 0.0 all-gather.5.cloned.1.call-update
  17.7 0.0 copy-start.1
  17.7 39.3 %all_to_all.30.in_ref = bf16[16,12,45,128]{3,2,1,0:T(8,128)(2,1)S(1)} all-to-all(bf16[16,12,45,128]{3,2,1,0:T(8,128)(2,1)} %get-tuple-element.10), channel_id=1, replica_groups=mesh['lat'=16,'chan'=8] {'lat'}, dimensions={0} | all-to-all | bytes 4423680 | tf_op jit(solution)/shard_map/all_to_all | solution.py:504
  57.0 0.0 copy-done.1
  57.0 6.8 %analysis.2 = bf16[128,40,128]{2,1,0:T(8,128)(2,1)} custom-call(s32[1]{0:T(128)} %bitcast.1.owner_ref, s32[192]{0:T(256)S(1)} %copy-done.1, bf16[16,12,45,128]{3,2,1,0:T(8,128)(2,1)S(1)} %all_to_all.30.in_ref, bf16[12,385,720]{2,1,0:T(8,128)(2,1)} %basis_ref.5), custom_call_target="tpu_custom_call" | custom-call | flops 6000000000 | bytes 1048576 | tf_op jit(solution)/shard_map/analysis/pallas_call | solution.py:300
  63.8 6.1 %all-to-all-start.1 = ((bf16[128,40,128]{2,1,0:T(8,128)(2,1)}), bf16[128,40,128]{2,1,0:T(8,128)(2,1)S(1)}, u32[]{:S(2)}, u32[]{:S(2)}) async-start(bf16[128,40,128]{2,1,0:T(8,128)(2,1)} %analysis.2), calls=%async_computation.1 | async-start | bytes 2621440 | tf_op jit(solution)/shard_map/all_to_all | solution.py:504
  69.9 0.0 all-gather.7.cloned.1.call-start
  70.0 21.9 %all-to-all-done.1.in_ref = bf16[128,40,128]{2,1,0:T(8,128)(2,1)S(1)} async-done(((bf16[128,40,128]{2,1,0:T(8,128)(2,1)}), bf16[128,40,128]{2,1,0:T(8,128)(2,1)S(1)}, u32[]{:S(2)}, u32[]{:S(2)}) %all-to-all-start.1) | async-done | bytes 1310752 | tf_op jit(solution)/shard_map/all_to_all | solution.py:504
  91.9 0.0 all-gather.5.cloned.1.call-done
  91.9 0.0 copy-start
  91.9 1.9 copy-done
  93.8 4.7 %spectral_filter.1 = (bf16[128,40,128]{2,1,0:T(8,128)(2,1)S(1)}, bf16[3,768,256]{2,1,0:T(8,128)(2,1)}) custom-call(s32[1]{0:T(128)} %bitcast.2.me_ref, bf16[128,40,128]{2,1,0:T(8,128)(2,1)S(1)} %all-to-all-done.1.in_ref, bf16[8,3,8,32,256]{4,3,2,1,0:T(8,128)(2,1)S(1)} %bitcast.11), custom_call_target="tpu_custom_call" | custom-call | flops 6000000000 | bytes 1048576 | tf_op jit(solution)/shard_map/spectral_filter/pallas_call | solution.py:437
  98.4 26.2 %all_to_all.31.in_ref = bf16[128,40,128]{2,1,0:T(8,128)(2,1)S(1)} all-to-all(bf16[128,40,128]{2,1,0:T(8,128)(2,1)S(1)} %get-tuple-element.12), channel_id=1, replica_groups=mesh['lat'=16,'chan'=8] {'lat','chan'}, dimensions={0} | all-to-all | bytes 2621440 | tf_op jit(solution)/shard_map/all_to_all | solution.py:504
  124.6 0.0 all-gather.7.cloned.1.call-update
  124.7 0.0 copy-start.2
  124.7 6.7 %synthesis.1 = bf16[16,12,45,128]{3,2,1,0:T(8,128)(2,1)S(1)} custom-call(s32[1]{0:T(128)} %bitcast.1.owner_ref, s32[192]{0:T(256)S(1)} %copy-done.1, bf16[128,40,128]{2,1,0:T(8,128)(2,1)S(1)} %all_to_all.31.in_ref, bf16[12,385,720]{2,1,0:T(8,128)(2,1)} %basis_ref.5), custom_call_target="tpu_custom_call" | custom-call | flops 7000000000 | bytes 1048576 | tf_op jit(solution)/shard_map/synthesis/pallas_call | solution.py:357
  131.4 0.0 slice-start
  131.4 34.3 %all_to_all.32.in_ref = bf16[16,12,45,128]{3,2,1,0:T(8,128)(2,1)S(1)} all-to-all(bf16[16,12,45,128]{3,2,1,0:T(8,128)(2,1)S(1)} %synthesis.1), channel_id=1, replica_groups=mesh['lat'=16,'chan'=8] {'lat'}, dimensions={0} | all-to-all | bytes 4423680 | tf_op jit(solution)/shard_map/all_to_all | solution.py:504
  165.7 0.0 copy-done.2
  165.7 0.0 slice-start.1
  165.7 18.7 %middle_transform.1 = (bf16[45,32,1440]{2,1,0:T(8,128)(2,1)}, bf16[16,12,45,128]{3,2,1,0:T(8,128)(2,1)S(1)}) custom-call(s32[192]{0:T(256)S(1)} %copy-done.1, bf16[16,12,45,128]{3,2,1,0:T(8,128)(2,1)S(1)} %all_to_all.32.in_ref, bf16[45,32,1440]{2,1,0:T(8,128)(2,1)} %bitcast.14, bf16[768,1440]{1,0:T(8,128)(2,1)S(1)} %copy-done.2), custom_call_target="tpu_custom_call" | custom-call | flops 24999999488 | bytes 1048576 | tf_op jit(solution)/shard_map/middle_transform/pallas_call | solution.py:204
  184.4 33.7 %all_to_all.33.in_ref = bf16[16,12,45,128]{3,2,1,0:T(8,128)(2,1)S(1)} all-to-all(bf16[16,12,45,128]{3,2,1,0:T(8,128)(2,1)S(1)} %get-tuple-element.16), channel_id=1, replica_groups=mesh['lat'=16,'chan'=8] {'lat'}, dimensions={0} | all-to-all | bytes 4423680 | tf_op jit(solution)/shard_map/all_to_all | solution.py:504
  218.1 0.0 slice-done
  218.1 0.0 slice-done.1
  218.1 4.8 %analysis.3 = bf16[16,12,24,128]{3,2,1,0:T(8,128)(2,1)} custom-call(s32[1]{0:T(128)} %bitcast.1.owner_ref, s32[192]{0:T(256)S(1)} %copy-done.1, bf16[16,12,45,128]{3,2,1,0:T(8,128)(2,1)S(1)} %all_to_all.33.in_ref, bf16[12,385,720]{2,1,0:T(8,128)(2,1)S(1)} %bitcast.10), custom_call_target="tpu_custom_call" | custom-call | flops 6000000000 | bytes 1048576 | tf_op jit(solution)/shard_map/analysis/pallas_call | solution.py:300
  222.9 3.7 %all-to-all-start.5 = ((bf16[16,12,24,128]{3,2,1,0:T(8,128)(2,1)}), bf16[16,12,24,128]{3,2,1,0:T(8,128)(2,1)S(1)}, u32[]{:S(2)}, u32[]{:S(2)}) async-start(bf16[16,12,24,128]{3,2,1,0:T(8,128)(2,1)} %analysis.3), calls=%async_computation.5 | async-start | bytes 2359296 | tf_op jit(solution)/shard_map/all_to_all | solution.py:504
  226.6 7.6 %fusion = bf16[1,45,32,1440]{3,2,1,0:T(8,128)(2,1)} fusion(bf16[45,32,1440]{2,1,0:T(8,128)(2,1)} %get-tuple-element.15, bf16[1,45,32,1440]{3,2,1,0:T(8,128)(2,1)} %param.8), kind=kLoop, calls=%fused_computation.1 | loop fusion | flops 8294400 | bytes 12441600 | tf_op jit(solution)/shard_map/broadcast_in_dim | solution.py:537
  234.2 10.0 %all-to-all-done.5.in_ref = bf16[16,12,24,128]{3,2,1,0:T(8,128)(2,1)S(1)} async-done(((bf16[16,12,24,128]{3,2,1,0:T(8,128)(2,1)}), bf16[16,12,24,128]{3,2,1,0:T(8,128)(2,1)S(1)}, u32[]{:S(2)}, u32[]{:S(2)}) %all-to-all-start.5) | async-done | bytes 1179680 | tf_op jit(solution)/shard_map/all_to_all | solution.py:504
  244.1 0.0 all-gather.7.cloned.1.call-done
  244.1 6.2 %filter_grad.1 = f32[24,32,256]{2,1,0:T(8,128)} custom-call(bf16[16,12,24,128]{3,2,1,0:T(8,128)(2,1)S(1)} %all-to-all-done.5.in_ref, bf16[8,3,768,256]{3,2,1,0:T(8,128)(2,1)} %bitcast.13), custom_call_target="tpu_custom_call" | custom-call | flops 6000000000 | bytes 1048576 | tf_op jit(solution)/shard_map/filter_grad/pallas_call | solution.py:483
  (1 shorter events, 0.0 us)
Async XLA Ops:
  7.2 84.7 %all-gather.5.cloned.1.call-start = ((), (), s32[]{:S(2)}) async-start(), calls=%async_computation.6 | async-start | bytes 3538944 | tf_op jit(solution)/shard_map/all_gather | solution.py:524
  17.7 39.4 %copy-start.1 = (s32[192]{0:T(256)S(1)}, s32[192]{0:T(256)}, u32[]{:S(2)}) copy-start(s32[192]{0:T(256)} %pair_ref.9) | copy-start | bytes 2308
  63.8 28.1 %all-to-all-start.1 = ((bf16[128,40,128]{2,1,0:T(8,128)(2,1)}), bf16[128,40,128]{2,1,0:T(8,128)(2,1)S(1)}, u32[]{:S(2)}, u32[]{:S(2)}) async-start(bf16[128,40,128]{2,1,0:T(8,128)(2,1)} %analysis.2), calls=%async_computation.1 | async-start | bytes 2621440 | tf_op jit(solution)/shard_map/all_to_all | solution.py:504
  69.9 174.2 %all-gather.7.cloned.1.call-start = ((), (), s32[]{:S(2)}) async-start(), calls=%async_computation.7 | async-start | bytes 10616832 | tf_op jit(solution)/shard_map/all_gather | solution.py:529
  91.9 1.9 copy-start
  124.7 41.0 %copy-start.2 = (bf16[768,1440]{1,0:T(8,128)(2,1)S(1)}, bf16[768,1440]{1,0:T(8,128)(2,1)}, u32[]{:S(2)}) copy-start(bf16[768,1440]{1,0:T(8,128)(2,1)} %constant.20.table_ref) | copy-start | bytes 6635524
  131.4 86.8 %slice-start = ((s8[7225344]{0:T(1024)(128)(4,1)}), s8[4194304]{0:T(1024)(128)(4,1)S(1)}, s32[]{:S(2)}) async-start(s8[7225344]{0:T(1024)(128)(4,1)} %bitcast.9), calls=%async_computation.8 | async-start | bytes 8388608
  165.7 52.5 %slice-start.1 = ((s8[7225344]{0:T(1024)(128)(4,1)}), s8[3031040]{0:T(1024)(128)(4,1)S(1)}, s32[]{:S(2)}) async-start(s8[7225344]{0:T(1024)(128)(4,1)} %bitcast.9), calls=%async_computation.9 | async-start | bytes 6062080
  222.9 21.2 %all-to-all-start.5 = ((bf16[16,12,24,128]{3,2,1,0:T(8,128)(2,1)}), bf16[16,12,24,128]{3,2,1,0:T(8,128)(2,1)S(1)}, u32[]{:S(2)}, u32[]{:S(2)}) async-start(bf16[16,12,24,128]{3,2,1,0:T(8,128)(2,1)} %analysis.3), calls=%async_computation.5 | async-start | bytes 2359296 | tf_op jit(solution)/shard_map/all_to_all | solution.py:504
Sparse Core Ops, SparseCore 0:
  17.8 30.1 all-gather.4
  124.8 49.8 all-gather.6
